TPU v7x, 256 devices: a whole 4x4x8 slice. The times are simulated.
256 devices in a mesh: seg: 8 (over x, core), space: 32 (over z, y).
Axes of the slice: x: 4, y: 4, z: 8, core: 2. Of those that a mesh axis runs over, the one named last changes fastest.
Arguments:
- tangents: float32 [8, 25, 3, 128, 8, 128], P('seg', None, None, 'space'), may hold values from -700 to 700
- base_flow: float32 [8, 4, 3, 128, 8, 128], P('seg', None, None, 'space'), may hold values from -4 to 4
- viscosity: float32 [8, 128, 8, 128], P('seg', 'space'), may hold values from 0.02 to 0.2
- source: float32 [8, 3, 128, 8, 128], P('seg', None, 'space'), may hold values from -6 to 6
Outputs:
- handed: float32 [8, 25, 3, 128, 8, 128], P('seg', None, None, 'space')
- growth: float32 [8, 24], P('seg')
- projection: float32 [8, 24], P('seg')
All inputs are finite; a program needn't handle non-finite values.
Results may differ from a plain program's by a relative error of at most 0.0003.
Values sent between devices are 32-bit elements; how exact they have to be, the bound alone decides.
A program may use at most 64 MiB of HBM per device.

v0:
```python
import jax
import jax.numpy as jnp
from jax import lax
from jax.sharding import PartitionSpec as P

DT = 0.5


def extended_2(x, sides, width):
    for axis, dim in sides:
        peers, length = (lax.axis_size(axis), x.shape[dim])
        up = [(i, (i + 1) % peers) for i in range(peers - 1)]
        down = [(j, i) for i, j in up]
        last = lax.slice_in_dim(x, length - width, length, axis=dim)
        first = lax.slice_in_dim(x, 0, width, axis=dim)
        before = lax.ppermute(last, axis, up)
        after = lax.ppermute(first, axis, down)
        x = jnp.concatenate([before, x, after], axis=dim)
    return x


def entering(value, axis, join, neutral):
    count, mine = (lax.axis_size(axis), lax.axis_index(axis))
    pieces = lax.all_gather(value, axis)
    so_far = jnp.full_like(value, 0) + jnp.asarray(neutral, value.dtype)

    def hop(position, so_far):
        longer = join(so_far, pieces[position])
        return jnp.where(position < mine, longer, so_far)

    return lax.fori_loop(0, count - 1, hop, so_far)


def shifted(x, axis, by):
    peers = lax.axis_size(axis)
    pairs = [(i, i + by) for i in range(peers) if 0 <= i + by < peers]
    return lax.ppermute(x, axis, pairs)


def pad_cross(tensor):
    widths = [(0, 0)] * (tensor.ndim - 2) + [(1, 1), (1, 1)]
    return jnp.pad(tensor, widths)


def neighbours(padded):
    centre = padded[..., 1:-1, 1:-1, 1:-1]
    neighbour_pairs = [
        (padded[..., 2:, 1:-1, 1:-1], padded[..., :-2, 1:-1, 1:-1]),
        (padded[..., 1:-1, 2:, 1:-1], padded[..., 1:-1, :-2, 1:-1]),
        (padded[..., 1:-1, 1:-1, 2:], padded[..., 1:-1, 1:-1, :-2]),
    ]
    return (centre, neighbour_pairs)


def advance(tangent_ext, flow_ext, viscous, forcing):
    centre, neighbour_pairs = neighbours(pad_cross(tangent_ext))
    flow_centre, flow_pairs = neighbours(pad_cross(flow_ext))
    transport = jnp.zeros_like(centre)
    product = jnp.zeros_like(centre)
    spread = -6.0 * centre
    for axis_number in range(3):
        forward, backward = neighbour_pairs[axis_number]
        flow_ahead, flow_behind = flow_pairs[axis_number]
        transport = transport + flow_centre[axis_number] * (0.5 * (forward - backward))
        flow_slope = 0.5 * (flow_ahead - flow_behind)
        product = product + centre[:, axis_number : axis_number + 1] * flow_slope[None]
        spread = spread + forward + backward
    tendency = -transport - product + viscous * spread
    updated = centre + DT * tendency
    driven = updated[-1:] + DT * forcing[None]
    return jnp.concatenate([updated[:-1], driven], axis=0)


def lower_cholesky(matrix):
    order = matrix.shape[0]
    places = jnp.arange(order)
    columns = []
    for column_index in range(order):
        accum = matrix[:, column_index]
        for earlier in range(column_index):
            accum = accum - columns[earlier] * columns[earlier][column_index]
        pivot = jnp.sqrt(accum[column_index])
        columns.append(jnp.where(places >= column_index, accum / pivot, jnp.zeros_like(accum)))
    return jnp.stack(columns, axis=1)


def lower_inverse(lower_factor):
    order = lower_factor.shape[0]
    identity_matrix = jnp.eye(order, dtype=lower_factor.dtype)
    rows = []
    for row_index in range(order):
        value = identity_matrix[row_index]
        if row_index > 0:
            value = value - jnp.dot(
                lower_factor[row_index, :row_index],
                jnp.stack(rows),
                precision=lax.Precision.HIGHEST,
            )
        rows.append(value / lower_factor[row_index, row_index])
    return jnp.stack(rows)


def combine_sum(earlier, later):
    return earlier + later


def body(tangents, base_flow, viscosity, source):
    current = tangents[0]
    flows = base_flow[0]
    viscous = viscosity[0]
    forcing = source[0]
    count_space = lax.axis_size("space")
    width_x = current.shape[2]
    cell_total = 3 * width_x * count_space * current.shape[3] * current.shape[4]
    sections = flows.shape[0]
    tangent_count = current.shape[0] - 1
    flow_halo = extended_2(flows, (("space", 2),), 1)
    for section_index in range(sections):
        extended = extended_2(current, (("space", 2),), 1)
        current = advance(extended, flow_halo[section_index], viscous, forcing)
    flattened = current.reshape(tangent_count + 1, -1)
    homogeneous = flattened[:tangent_count]
    driven = flattened[tangent_count]
    local_gram = jnp.dot(homogeneous, homogeneous.T, precision=lax.Precision.HIGHEST) / cell_total
    gram_matrix = lax.psum(local_gram, "space")
    lower_factor = lower_cholesky(gram_matrix)
    inverse_lower = lower_inverse(lower_factor)
    orthonormal = jnp.dot(inverse_lower, homogeneous, precision=lax.Precision.HIGHEST)
    local_inner = jnp.dot(orthonormal, driven, precision=lax.Precision.HIGHEST) / cell_total
    projection = lax.psum(local_inner, "space")
    remainder = driven - jnp.dot(projection, orthonormal, precision=lax.Precision.HIGHEST)
    log_growth = jnp.log(jnp.diagonal(lower_factor))
    earlier_sum = entering(log_growth, "seg", combine_sum, jnp.zeros_like(log_growth))
    growth = earlier_sum + log_growth
    processed = jnp.concatenate([orthonormal, remainder[None]], axis=0).reshape(current.shape)
    received = shifted(processed, "seg", 1)
    handed = jnp.where(lax.axis_index("seg") == 0, tangents[0], received)
    return (handed[None], growth[None], projection[None])


def solution(mesh):
    return jax.shard_map(
        body,
        mesh=mesh,
        in_specs=(
            P("seg", None, None, "space", None, None),
            P("seg", None, None, "space", None, None),
            P("seg", "space", None, None),
            P("seg", None, "space", None, None),
        ),
        out_specs=(P("seg", None, None, "space", None, None), P("seg", None), P("seg", None)),
        check_vma=False,
    )
```

profile of v0, /device:TPU:1, one launch (start us, length us, event | category | flops | bytes accessed | tf_op | source)
XLA Modules:
  0.0 776.7 jit_solution(5817831969670078572)
XLA Ops:
  4.9 5.4 collective-permute-start.1
  78.1 124.0 %psum.14 = f32[24,24]{0,1:T(8,128)S(1)} all-reduce(f32[24,24]{0,1:T(8,128)S(1)} %fusion.7), channel_id=1, replica_groups=mesh['seg'=8,'space'=32] {'space'}, use_global_device_ids=true, to_apply=%region_0.1 | all-reduce | flops 576 | bytes 4608 | tf_op jit(solution)/shard_map/psum | solution.py:125
  245.6 5.8 multiply_subtract_fusion.14
  253.4 6.1 multiply_subtract_fusion.13
  261.5 6.9 multiply_subtract_fusion.12
  269.7 40.6 %compare_select_fusion.24 = (f32[24,1]{0,1:T(1,128)S(1)}, f32[24,1]{0,1:T(1,128)S(1)}, f32[24,1]{0,1:T(1,128)S(1)}, f32[24,1]{0,1:T(1,128)S(1)}, f32[24,1]{0,1:T...) fusion(f32[]{:T(128)} %bitcast.161, ...), kind=kLoop, calls=%fused_computation.331 | loop fusion | flops 3912 | bytes 2416 | tf_op jit(solution)/shard_map/jit(_where)/select_n | solution.py:83
  311.1 7.4 multiply_subtract_fusion.11
  320.4 8.3 %multiply_subtract_fusion.10 = f32[24]{0:T(128)S(1)} fusion(f32[]{:T(128)} %bitcast.197, f32[]{:T(128)} %bitcast.196, f32[]{:T(128)} %bitcast.195, f32[]{:T(128)} %bitcast.194, f32[]{:T(128)} %bitcast.193, f32[]{:T(128)} %bitcast.192, f32[]{:T(128)} %bitcast.191, f32[]{:T(128)} %bitcast.190, f32[]{:T(128)} %bitcast.189, f32[]{:T(128)} %bitcast.188, ...), kind=kLoop, calls=%fused_computation.523 | loop fusion | flops 1488 | bytes 1540 | tf_op jit(solution)/shard_map/sub | solution.py:81
  330.8 8.7 %multiply_subtract_fusion.9 = f32[24]{0:T(128)S(1)} fusion(f32[]{:T(128)} %bitcast.217, f32[]{:T(128)} %bitcast.216, f32[]{:T(128)} %bitcast.215, f32[]{:T(128)} %bitcast.214, f32[]{:T(128)} %bitcast.213, f32[]{:T(128)} %bitcast.212, f32[]{:T(128)} %bitcast.211, f32[]{:T(128)} %bitcast.210, f32[]{:T(128)} %bitcast.209, f32[]{:T(128)} %bitcast.208, ...), kind=kLoop, calls=%fused_computation.522 | loop fusion | flops 1608 | bytes 1644 | tf_op jit(solution)/shard_map/sub | solution.py:81
  341.5 9.2 %multiply_subtract_fusion.8 = f32[24]{0:T(128)S(1)} fusion(f32[]{:T(128)} %bitcast.238, f32[]{:T(128)} %bitcast.237, f32[]{:T(128)} %bitcast.236, f32[]{:T(128)} %bitcast.235, f32[]{:T(128)} %bitcast.234, f32[]{:T(128)} %bitcast.233, f32[]{:T(128)} %bitcast.232, f32[]{:T(128)} %bitcast.231, f32[]{:T(128)} %bitcast.230, f32[]{:T(128)} %bitcast.229, ...), kind=kLoop, calls=%fused_computation.521 | loop fusion | flops 1728 | bytes 1748 | tf_op jit(solution)/shard_map/sub | solution.py:81
  352.7 10.1 %multiply_subtract_fusion.7 = f32[24]{0:T(128)S(1)} fusion(f32[]{:T(128)} %bitcast.260, f32[]{:T(128)} %bitcast.259, f32[]{:T(128)} %bitcast.258, f32[]{:T(128)} %bitcast.257, f32[]{:T(128)} %bitcast.256, f32[]{:T(128)} %bitcast.255, f32[]{:T(128)} %bitcast.254, f32[]{:T(128)} %bitcast.253, f32[]{:T(128)} %bitcast.252, f32[]{:T(128)} %bitcast.251, ...), kind=kLoop, calls=%fused_computation.520 | loop fusion | flops 1848 | bytes 1852 | tf_op jit(solution)/shard_map/sub | solution.py:81
  364.9 10.7 %multiply_subtract_fusion.6 = f32[24]{0:T(128)S(1)} fusion(f32[]{:T(128)} %bitcast.283, f32[]{:T(128)} %bitcast.282, f32[]{:T(128)} %bitcast.281, f32[]{:T(128)} %bitcast.280, f32[]{:T(128)} %bitcast.279, f32[]{:T(128)} %bitcast.278, f32[]{:T(128)} %bitcast.277, f32[]{:T(128)} %bitcast.276, f32[]{:T(128)} %bitcast.275, f32[]{:T(128)} %bitcast.274, ...), kind=kLoop, calls=%fused_computation.519 | loop fusion | flops 1968 | bytes 1956 | tf_op jit(solution)/shard_map/sub | solution.py:81
  377.5 10.8 %multiply_subtract_fusion.5 = f32[24]{0:T(128)S(1)} fusion(f32[]{:T(128)} %bitcast.307, f32[]{:T(128)} %bitcast.306, f32[]{:T(128)} %bitcast.305, f32[]{:T(128)} %bitcast.304, f32[]{:T(128)} %bitcast.303, f32[]{:T(128)} %bitcast.302, f32[]{:T(128)} %bitcast.301, f32[]{:T(128)} %bitcast.300, f32[]{:T(128)} %bitcast.299, f32[]{:T(128)} %bitcast.298, ...), kind=kLoop, calls=%fused_computation.518 | loop fusion | flops 2088 | bytes 2060 | tf_op jit(solution)/shard_map/sub | solution.py:81
  390.2 11.9 %multiply_subtract_fusion.4 = f32[24]{0:T(128)S(1)} fusion(f32[]{:T(128)} %bitcast.332, f32[]{:T(128)} %bitcast.331, f32[]{:T(128)} %bitcast.330, f32[]{:T(128)} %bitcast.329, f32[]{:T(128)} %bitcast.328, f32[]{:T(128)} %bitcast.327, f32[]{:T(128)} %bitcast.326, f32[]{:T(128)} %bitcast.325, f32[]{:T(128)} %bitcast.324, f32[]{:T(128)} %bitcast.323, ...), kind=kLoop, calls=%fused_computation.517 | loop fusion | flops 2208 | bytes 2164 | tf_op jit(solution)/shard_map/sub | solution.py:81
  404.2 12.6 %multiply_subtract_fusion.3 = f32[24]{0:T(128)S(1)} fusion(f32[]{:T(128)} %bitcast.358, f32[]{:T(128)} %bitcast.357, f32[]{:T(128)} %bitcast.356, f32[]{:T(128)} %bitcast.355, f32[]{:T(128)} %bitcast.354, f32[]{:T(128)} %bitcast.353, f32[]{:T(128)} %bitcast.352, f32[]{:T(128)} %bitcast.351, f32[]{:T(128)} %bitcast.350, f32[]{:T(128)} %bitcast.349, ...), kind=kLoop, calls=%fused_computation.516 | loop fusion | flops 2328 | bytes 2268 | tf_op jit(solution)/shard_map/sub | solution.py:81
  418.8 13.2 %multiply_subtract_fusion.2 = f32[24]{0:T(128)S(1)} fusion(f32[]{:T(128)} %bitcast.385, f32[]{:T(128)} %bitcast.384, f32[]{:T(128)} %bitcast.383, f32[]{:T(128)} %bitcast.382, f32[]{:T(128)} %bitcast.381, f32[]{:T(128)} %bitcast.380, f32[]{:T(128)} %bitcast.379, f32[]{:T(128)} %bitcast.378, f32[]{:T(128)} %bitcast.377, f32[]{:T(128)} %bitcast.376, ...), kind=kLoop, calls=%fused_computation.515 | loop fusion | flops 2448 | bytes 2372 | tf_op jit(solution)/shard_map/sub | solution.py:81
  434.0 13.9 %multiply_subtract_fusion.1 = (f32[24]{0:T(128)S(1)}, f32[24,1]{0,1:T(1,128)S(1)}) fusion(f32[]{:T(128)} %bitcast.413, f32[]{:T(128)} %bitcast.412, f32[]{:T(128)} %bitcast.411, f32[]{:T(128)} %bitcast.410, f32[]{:T(128)} %bitcast.409, f32[]{:T(128)} %bitcast.408, f32[]{:T(128)} %bitcast.407, f32[]{:T(128)} %bitcast.406, f32[]{:T(128)} %bitcast.405, ...), kind=kLoop, calls=%fused_computation.514 | loop fusion | flops 2568 | bytes 2572 | tf_op jit(solution)/shard_map/sub | solution.py:81
  449.9 14.1 %multiply_subtract_fusion = f32[24]{0:T(128)S(1)} fusion(f32[]{:T(128)} %bitcast.442, f32[]{:T(128)} %bitcast.441, f32[]{:T(128)} %bitcast.440, f32[]{:T(128)} %bitcast.439, f32[]{:T(128)} %bitcast.438, f32[]{:T(128)} %bitcast.437, f32[]{:T(128)} %bitcast.436, f32[]{:T(128)} %bitcast.435, f32[]{:T(128)} %bitcast.434, f32[]{:T(128)} %bitcast.433, ...), kind=kLoop, calls=%fused_computation.513 | loop fusion | flops 2688 | bytes 2580 | tf_op jit(solution)/shard_map/sub | solution.py:81
  465.4 130.5 %compare_select_fusion = (f32[24,1]{0,1:T(1,128)S(1)}, f32[24,1]{0,1:T(1,128)S(1)}, f32[24,1]{0,1:T(1,128)S(1)}, f32[24,1]{0,1:T(1,128)S(1)}, f32[24,1]{0,1:T(1,...) fusion(f32[24,1]{0,1:T(1,128)S(1)} %get-tuple-element.137, ...), kind=kLoop, calls=%fused_computation.307 | loop fusion | flops 10968 | bytes 4248 | tf_op jit(solution)/shard_map/jit(_where)/select_n | solution.py:83
  595.9 13.2 %compare_select_fusion.2 = f32[24,1]{0,1:T(1,128)S(1)} fusion(f32[24,1]{0,1:T(1,128)S(1)} %get-tuple-element.125, f32[24,1]{0,1:T(1,128)S(1)} %get-tuple-element.126, f32[24,1]{0,1:T(1,128)S(1)} %get-tuple-element.127, f32[24,1]{0,1:T(1,128)S(1)} %get-tuple-element.128, f32[24,1]{0,1:T(1,128)S(1)} %get-tuple-element.129, ...), kind=kLoop, calls=%fused_computation.309 | loop fusion | flops 1128 | bytes 2296 | tf_op jit(solution)/shard_map/jit(_where)/select_n | solution.py:83
  611.8 45.1 %all-reduce.8 = f32[192]{0:T(256)S(1)} all-reduce(f32[192]{0:T(256)S(1)} %log_dynamic-update-slice_fusion), channel_id=2, replica_groups=mesh['seg'=8,'space'=32] {'seg'}, use_global_device_ids=true, to_apply=%add.8 | all-reduce | flops 192 | bytes 1536
  686.8 55.7 %psum.15 = f32[24]{0:T(128)S(1)} all-reduce(f32[24]{0:T(128)S(1)} %fusion.53), channel_id=1, replica_groups=mesh['seg'=8,'space'=32] {'space'}, use_global_device_ids=true, to_apply=%region_1.2 | all-reduce | flops 24 | bytes 192 | tf_op jit(solution)/shard_map/psum | solution.py:130
  744.4 15.1 %collective-permute-start.10 = (f32[25,3,4,8,128]{4,3,2,1,0:T(8,128)}, f32[25,3,4,8,128]{4,3,2,1,0:T(8,128)S(1)}, u32[]{:S(2)}, u32[]{:S(2)}) collective-permute-start(f32[25,3,4,8,128]{4,3,2,1,0:T(8,128)} %pad_maximum_fusion.17), channel_id=1, source_target_pairs={{0,32},{32,64},{64,96},{96,128},{128,160},{160,192},{192,224},{1,3... | collective-permute-start | bytes 3686408 | tf_op jit(solution)/shard_map/ppermute | solution.py:37
  760.4 13.2 %collective-permute-done.10 = f32[25,3,4,8,128]{4,3,2,1,0:T(8,128)S(1)} collective-permute-done((f32[25,3,4,8,128]{4,3,2,1,0:T(8,128)}, f32[25,3,4,8,128]{4,3,2,1,0:T(8,128)S(1)}, u32[]{:S(2)}, u32[]{:S(2)}) %collective-permute-start.10) | collective-permute-done | bytes 1228832 | tf_op jit(solution)/shard_map/ppermute | solution.py:37
  (268 shorter events, 165.7 us)
Async XLA Ops:
  0.6 9.7 %copy-start.2 = (f32[1,4,3,4,8,128]{5,4,3,2,1,0:T(8,128)S(1)}, f32[1,4,3,4,8,128]{5,4,3,2,1,0:T(8,128)}, u32[]{:S(2)}) copy-start(f32[1,4,3,4,8,128]{5,4,3,2,1,0:T(8,128)} %param.7) | copy-start | bytes 589828
  3.6 17.2 %collective-permute-start = (f32[25,3,1,8,128]{4,0,3,2,1:T(8,128)}, f32[25,3,1,8,128]{4,0,3,2,1:T(8,128)S(1)}, u32[]{:S(2)}, u32[]{:S(2)}) collective-permute-start(f32[25,3,1,8,128]{4,0,3,2,1:T(8,128)} %get-tuple-element.155), channel_id=1, source_target_pairs={{1,0},{2,1},{3,2},{4,3},{5,4},{6,5},{7,6},{8,7},{9,8},{10,9},{11,1... | collective-permute-start | bytes 921608 | tf_op jit(solution)/shard_map/ppermute | solution.py:17
  4.9 15.9 %collective-permute-start.1 = (f32[25,3,1,8,128]{4,0,3,2,1:T(8,128)}, f32[25,3,1,8,128]{4,0,3,2,1:T(8,128)}, u32[]{:S(2)}, u32[]{:S(2)}) collective-permute-start(f32[25,3,1,8,128]{4,0,3,2,1:T(8,128)} %get-tuple-element.154), channel_id=1, source_target_pairs={{0,1},{1,2},{2,3},{3,4},{4,5},{5,6},{6,7},{7,8},{8,9},{9,10},{10,1... | collective-permute-start | bytes 921608 | tf_op jit(solution)/shard_map/ppermute | solution.py:16
  11.0 6.6 collective-permute-start.2
  14.2 5.1 collective-permute-start.3
  20.8 3.3 copy-start.3
  27.1 0.8 copy-start.1
  28.0 11.9 %collective-permute-start.4 = (f32[25,3,1,8,128]{4,0,3,2,1:T(8,128)S(1)}, f32[25,3,1,8,128]{4,0,3,2,1:T(8,128)S(1)}, u32[]{:S(2)}, u32[]{:S(2)}) collective-permute-start(f32[25,3,1,8,128]{4,0,3,2,1:T(8,128)S(1)} %get-tuple-element.170), channel_id=1, source_target_pairs={{1,0},{2,1},{3,2},{4,3},{5,4},{6,5},{7,6},{8,7},{9,8},{10,9},{11,1... | collective-permute-start | bytes 921608 | tf_op jit(solution)/shard_map/ppermute | solution.py:17
  29.3 11.5 %collective-permute-start.5 = (f32[25,3,1,8,128]{4,0,3,2,1:T(8,128)S(1)}, f32[25,3,1,8,128]{4,0,3,2,1:T(8,128)S(1)}, u32[]{:S(2)}, u32[]{:S(2)}) collective-permute-start(f32[25,3,1,8,128]{4,0,3,2,1:T(8,128)S(1)} %get-tuple-element.169), channel_id=1, source_target_pairs={{0,1},{1,2},{2,3},{3,4},{4,5},{5,6},{6,7},{7,8},{8,9},{9,10},{10,1... | collective-permute-start | bytes 921608 | tf_op jit(solution)/shard_map/ppermute | solution.py:16
  45.5 10.5 %collective-permute-start.6 = (f32[25,3,1,8,128]{4,0,3,2,1:T(8,128)S(1)}, f32[25,3,1,8,128]{4,0,3,2,1:T(8,128)S(1)}, u32[]{:S(2)}, u32[]{:S(2)}) collective-permute-start(f32[25,3,1,8,128]{4,0,3,2,1:T(8,128)S(1)} %get-tuple-element.165), channel_id=1, source_target_pairs={{1,0},{2,1},{3,2},{4,3},{5,4},{6,5},{7,6},{8,7},{9,8},{10,9},{11,1... | collective-permute-start | bytes 921608 | tf_op jit(solution)/shard_map/ppermute | solution.py:17
  46.8 10.1 %collective-permute-start.7 = (f32[25,3,1,8,128]{4,0,3,2,1:T(8,128)S(1)}, f32[25,3,1,8,128]{4,0,3,2,1:T(8,128)S(1)}, u32[]{:S(2)}, u32[]{:S(2)}) collective-permute-start(f32[25,3,1,8,128]{4,0,3,2,1:T(8,128)S(1)} %get-tuple-element.164), channel_id=1, source_target_pairs={{0,1},{1,2},{2,3},{3,4},{4,5},{5,6},{6,7},{7,8},{8,9},{9,10},{10,1... | collective-permute-start | bytes 921608 | tf_op jit(solution)/shard_map/ppermute | solution.py:16
  61.6 9.6 %collective-permute-start.8 = (f32[25,3,1,8,128]{4,0,3,2,1:T(8,128)S(1)}, f32[25,3,1,8,128]{4,0,3,2,1:T(8,128)S(1)}, u32[]{:S(2)}, u32[]{:S(2)}) collective-permute-start(f32[25,3,1,8,128]{4,0,3,2,1:T(8,128)S(1)} %get-tuple-element.160), channel_id=1, source_target_pairs={{1,0},{2,1},{3,2},{4,3},{5,4},{6,5},{7,6},{8,7},{9,8},{10,9},{11,1... | collective-permute-start | bytes 921608 | tf_op jit(solution)/shard_map/ppermute | solution.py:17
  62.9 9.4 %collective-permute-start.9 = (f32[25,3,1,8,128]{4,0,3,2,1:T(8,128)S(1)}, f32[25,3,1,8,128]{4,0,3,2,1:T(8,128)S(1)}, u32[]{:S(2)}, u32[]{:S(2)}) collective-permute-start(f32[25,3,1,8,128]{4,0,3,2,1:T(8,128)S(1)} %get-tuple-element.159), channel_id=1, source_target_pairs={{0,1},{1,2},{2,3},{3,4},{4,5},{5,6},{6,7},{7,8},{8,9},{9,10},{10,1... | collective-permute-start | bytes 921608 | tf_op jit(solution)/shard_map/ppermute | solution.py:16
  742.5 1.9 copy-start.5
  743.3 16.3 %copy-start.4 = (f32[24]{0:T(128)S(1)}, f32[24]{0:T(128)}, u32[]{:S(2)}) copy-start(f32[24]{0:T(128)} %custom-call.2) | copy-start | bytes 292
  743.3 30.3 %copy-start = (f32[1,25,3,4,8,128]{5,4,3,2,1,0:T(8,128)S(1)}, f32[1,25,3,4,8,128]{5,4,3,2,1,0:T(8,128)}, u32[]{:S(2)}) copy-start(f32[1,25,3,4,8,128]{5,4,3,2,1,0:T(8,128)} %param.6) | copy-start | bytes 3686404
  744.4 29.1 %collective-permute-start.10 = (f32[25,3,4,8,128]{4,3,2,1,0:T(8,128)}, f32[25,3,4,8,128]{4,3,2,1,0:T(8,128)S(1)}, u32[]{:S(2)}, u32[]{:S(2)}) collective-permute-start(f32[25,3,4,8,128]{4,3,2,1,0:T(8,128)} %pad_maximum_fusion.17), channel_id=1, source_target_pairs={{0,32},{32,64},{64,96},{96,128},{128,160},{160,192},{192,224},{1,3... | collective-permute-start | bytes 3686408 | tf_op jit(solution)/shard_map/ppermute | solution.py:37
where the time goes:
time: 785 us; the launch traced here: 777 us
  other arithmetic  384 us (49%)
  blocking collectives  225 us (29%)
  local copies, waits for them, and re-layouts  51.2 us (7%)
  starting transfers between devices  44.9 us (6%)
  waiting for transfers between devices  30.6 us (4%)
  matrix products  22.8 us (3%)
  between operations  18.5 us (2%)
    select_n x27, other arithmetic, lower_cholesky(): jnp.where(places >= column_index, accum / pivot, jnp.zeros_like(accum))  184 us
    sub x23, other arithmetic, lower_cholesky(): accum = accum - columns[earlier] * columns[earlier][column_index]  172 us
    psum x1, blocking collectives, body(): gram_matrix = lax.psum(local_gram, 'space')  124 us
    psum x1, blocking collectives, body(): projection = lax.psum(local_inner, 'space')  55.7 us
    unnamed x1, blocking collectives  45.1 us
    ppermute x5, starting transfers between devices, extended_2(): before = lax.ppermute(last, axis, up)  23.4 us
    dot_general x22, matrix products, lower_inverse(): jnp.dot(lower_factor[row_index, :row_index], jnp.stack(rows), precision=l...  16.6 us
  transfers between devices with their start and end apart: 11, of which 8 were waited for; matrix products, arithmetic and copies ran while one was open for 1% of the time, Pallas kernels for 0%

commit v1 on v0

v1 whole, which is shorter than its diff:
```python
import functools

import jax
import jax.numpy as jnp
from jax import lax
from jax.experimental import pallas as pl
from jax.experimental.pallas import tpu as pltpu
from jax.sharding import PartitionSpec as P

MESH = pl.DeviceIdType.MESH
DT = 0.5
ROW = 4
SLAB = 4
WIDE = 3 * SLAB
STEPS = 4
AHEAD = 4


def signs(shape, dim):
    return lax.broadcasted_iota(jnp.int32, shape, dim)


def coefficients(s, flowx, viscx, srcx, coef, position, planes_total):
    lo, hi = s + 1, WIDE - 1 - s
    n = hi - lo
    first = position * SLAB - SLAB
    plane = first + lo - 1 + signs((n + 2, 8, 128), 0)
    inside = (plane >= 0) & (plane < planes_total)
    ahead_in, behind_in = inside[2:], inside[:n]
    rows, lanes = signs((n, 8, 128), 1), signs((n, 8, 128), 2)
    hn = DT * viscx[lo:hi]
    u = []
    for d in range(3):
        u.append(jnp.where(inside, flowx[s, d, lo - 1 : hi + 1], 0.0))
    hu = [(0.5 * DT) * u[d][1 : n + 1] for d in range(3)]
    coef[s, 0, lo:hi] = jnp.where(ahead_in, hn - hu[0], 0.0)
    coef[s, 1, lo:hi] = jnp.where(behind_in, hn + hu[0], 0.0)
    coef[s, 2, lo:hi] = jnp.where(rows < 7, hn - hu[1], 0.0)
    coef[s, 3, lo:hi] = jnp.where(rows > 0, hn + hu[1], 0.0)
    coef[s, 4, lo:hi] = jnp.where(lanes < 127, hn - hu[2], 0.0)
    coef[s, 5, lo:hi] = jnp.where(lanes > 0, hn + hu[2], 0.0)
    centre = 1.0 - 6.0 * hn
    for c in range(3):
        uc = u[c][1 : n + 1]
        slope = [
            u[c][2:] - u[c][:n],
            jnp.where(rows < 7, pltpu.roll(uc, 7, 1), 0.0)
            - jnp.where(rows > 0, pltpu.roll(uc, 1, 1), 0.0),
            jnp.where(lanes < 127, pltpu.roll(uc, 127, 2), 0.0)
            - jnp.where(lanes > 0, pltpu.roll(uc, 1, 2), 0.0),
        ]
        for d in range(3):
            local = (-0.5 * DT) * slope[d]
            if c == d:
                local = centre + local
            coef[s, 6 + 3 * c + d, lo:hi] = local


def step(s, src, dst, coef, base):
    lo, hi = s + 1, WIDE - 1 - s
    w = [src[c, lo:hi] for c in range(3)]
    k = [coef[s, i, lo:hi] for i in range(6)]
    for c in range(3):
        new = k[0] * src[c, lo + 1 : hi + 1] + k[1] * src[c, lo - 1 : hi - 1]
        new += k[2] * pltpu.roll(w[c], 7, 1) + k[3] * pltpu.roll(w[c], 1, 1)
        new += k[4] * pltpu.roll(w[c], 127, 2) + k[5] * pltpu.roll(w[c], 1, 2)
        for d in range(3):
            new += coef[s, 6 + 3 * c + d, lo:hi] * w[d]
        dst[c, lo - base : hi - base] = new


def eliminate(gram, count):
    rows, lanes = signs((32, 128), 0), signs((32, 128), 1)
    a = jnp.where(lanes == rows + 32, 1.0, gram)
    for j in range(count):
        row = a[j : j + 1, :]
        m = jnp.where(rows > j, a[:, j : j + 1] * (1.0 / a[j : j + 1, j : j + 1]), 0.0)
        a = a - m * row
    diagonal = jnp.where(lanes == rows, a, 0.0)
    pivots = jnp.sum(diagonal, axis=1, keepdims=True)
    scale = jnp.where(rows[:, :1] < count, 1.0 / jnp.sqrt(pivots), 1.0)
    return a, diagonal, scale


def kernel(
    sizes,
    tang, flow, visc, src,
    handed, growth, proj,
    ext, flowx, viscx, srcx, coef, tmp_a, tmp_b, stepped, prev, outv,
    accs, gram, spread, part_y, part_z, part_p, logs,
    local_sems, halo_send, halo_recv, side_send, side_recv,
    shift_send, shift_recv, y_send, y_recv, z_send, z_recv, p_send, p_recv,
    log_send, log_recv, out_sems,
):
    n_seg, n_space, count = sizes
    total = count + 1
    depth = n_space // ROW
    seg, pos = lax.axis_index("seg"), lax.axis_index("space")
    y, z = lax.rem(pos, ROW), pos // ROW
    right = (seg, lax.rem(pos + 1, n_space))
    left = (seg, lax.rem(pos + n_space - 1, n_space))

    def along_y(d):
        return (seg, z * ROW + lax.rem(y + d, ROW))

    def along_z(d, ds=0):
        return (lax.rem(seg + ds, n_seg), lax.rem(z + d, depth) * ROW + y)

    def along_seg(d):
        return (lax.rem(seg + d, n_seg), pos)

    senders = [left, right]
    senders += [along_y(d) for d in range(1, ROW)]
    senders += [along_z(d) for d in range(1, depth)]
    senders += [along_z(d, n_seg - 1) for d in range(1, depth)]
    senders += [along_seg(d) for d in range(1, n_seg)]
    barrier = pltpu.get_barrier_semaphore()
    for device in senders:
        pl.semaphore_signal(barrier, inc=1, device_id=device, device_id_type=MESH)

    own = pl.ds(SLAB, SLAB)
    locals_ = [
        pltpu.make_async_copy(tang.at[0], ext.at[:, :, own], local_sems.at[0]),
        pltpu.make_async_copy(flow.at[0], flowx.at[:, :, own], local_sems.at[1]),
        pltpu.make_async_copy(visc.at[0], viscx.at[own], local_sems.at[2]),
        pltpu.make_async_copy(src.at[0], srcx.at[:, own], local_sems.at[3]),
    ]
    for copy in locals_:
        copy.start()
    stepped[...] = jnp.zeros_like(stepped)
    gram[...] = jnp.zeros_like(gram)

    def remote(a, b, send, recv, device):
        return pltpu.make_async_remote_copy(
            src_ref=a, dst_ref=b, send_sem=send, recv_sem=recv,
            device_id=device, device_id_type=MESH,
        )

    def halo(k):
        return [
            remote(tang.at[0, k], ext.at[k, :, pl.ds(0, SLAB)],
                   halo_send.at[0, k], halo_recv.at[0, k], right),
            remote(tang.at[0, k], ext.at[k, :, pl.ds(2 * SLAB, SLAB)],
                   halo_send.at[1, k], halo_recv.at[1, k], left),
        ]

    sides = []
    for s in range(STEPS):
        n = SLAB - s
        sides.append(remote(flow.at[0, s, :, pl.ds(s, n)], flowx.at[s, :, pl.ds(s, n)],
                            side_send.at[0, s], side_recv.at[0, s], right))
        sides.append(remote(flow.at[0, s, :, pl.ds(0, n)], flowx.at[s, :, pl.ds(2 * SLAB, n)],
                            side_send.at[1, s], side_recv.at[1, s], left))
    n = SLAB - 1
    sides.append(remote(visc.at[0, pl.ds(1, n)], viscx.at[pl.ds(1, n)],
                        side_send.at[0, 4], side_recv.at[0, 4], right))
    sides.append(remote(visc.at[0, pl.ds(0, n)], viscx.at[pl.ds(2 * SLAB, n)],
                        side_send.at[1, 4], side_recv.at[1, 4], left))
    sides.append(remote(src.at[0, :, pl.ds(1, n)], srcx.at[:, pl.ds(1, n)],
                        side_send.at[0, 5], side_recv.at[0, 5], right))
    sides.append(remote(src.at[0, :, pl.ds(0, n)], srcx.at[:, pl.ds(2 * SLAB, n)],
                        side_send.at[1, 5], side_recv.at[1, 5], left))

    pl.semaphore_wait(barrier, len(senders))
    for copy in sides:
        copy.start()
    for k in range(AHEAD):
        for copy in halo(k):
            copy.start()
    for copy in locals_:
        copy.wait()
    for copy in sides:
        copy.wait_recv()
    for s in range(STEPS):
        coefficients(s, flowx, viscx, srcx, coef, pos, n_space * SLAB)

    def shift(k):
        return remote(stepped.at[k], prev.at[k], shift_send.at[k], shift_recv.at[k], along_seg(1))

    rows, lanes = signs((32, 128), 0), signs((32, 128), 1)

    def one(k, carry):
        for copy in halo(k):
            copy.wait_recv()

        @pl.when(k + AHEAD < total)
        def _():
            for copy in halo(k + AHEAD):
                copy.start()

        chain = [ext.at[k], tmp_a, tmp_b, tmp_a, stepped.at[k]]
        for s in range(STEPS):
            final = s == STEPS - 1
            step(s, chain[s], chain[s + 1], coef, SLAB if final else 0)

            @pl.when(k == count)
            def _():
                lo, hi = s + 1, WIDE - 1 - s
                base = SLAB if final else 0
                dst = chain[s + 1]
                for c in range(3):
                    dst[c, lo - base : hi - base] = dst[c, lo - base : hi - base] + DT * srcx[c, lo:hi]

        shift(k).start()
        w = stepped[k]
        for j in range(total):
            accs[8 * j : 8 * j + 8, :] = jnp.sum(w * stepped[j], axis=(0, 1))
        folded = accs[pl.ds(0, 32, stride=8), :]
        for i in range(1, 8):
            folded += accs[pl.ds(i, 32, stride=8), :]
        column = jnp.sum(folded, axis=1, keepdims=True)
        row = jnp.sum(jnp.where(rows == lanes, column, 0.0), axis=0, keepdims=True)
        g = gram[...]
        g = jnp.where((lanes == k) & (rows <= k), column, g)
        g = jnp.where((rows == k) & (lanes <= k), row, g)
        gram[...] = g
        return carry

    accs[8 * total :, :] = jnp.zeros((8 * (32 - total), 128), jnp.float32)
    lax.fori_loop(0, total, one, 0)

    cells = 3 * SLAB * 8 * 128 * n_space
    packed = gram[0:8, :]
    for i in range(1, 4):
        packed += pltpu.roll(gram[8 * i : 8 * i + 8, :], 32 * i, 1)
    part_y[y] = packed * (1.0 / cells)

    def exchange_y(d):
        return remote(part_y.at[y], part_y.at[y], y_send.at[d], y_recv.at[y], along_y(d))

    def exchange_z(d):
        return remote(part_z.at[z], part_z.at[z], z_send.at[d], z_recv.at[z], along_z(d))

    def exchange_p(d):
        return remote(part_z.at[z], part_p.at[z], p_send.at[d], p_recv.at[z], along_z(d, 1))

    def arrived(slot, sems, position):
        remote(slot.at[position], slot.at[position], y_send.at[0], sems.at[position], left).wait_recv()

    for d in range(1, ROW):
        exchange_y(d).start()
    for d in range(1, ROW):
        arrived(part_y, y_recv, lax.rem(y + d, ROW))
    part_z[z] = part_y[0] + part_y[1] + part_y[2] + part_y[3]
    for d in range(1, depth):
        exchange_z(d).start()
    for d in range(depth):
        exchange_p(d).start()
    for d in range(1, depth):
        arrived(part_z, z_recv, lax.rem(z + d, depth))
    for d in range(depth):
        arrived(part_p, p_recv, lax.rem(z + d, depth))

    def unpack(slots):
        sums = slots[0]
        for i in range(1, depth):
            sums = sums + slots[i]
        narrow = signs((8, 128), 1) < 32
        pieces = [jnp.where(narrow, sums, 0.0)]
        for i in range(1, 4):
            pieces.append(jnp.where(narrow, pltpu.roll(sums, 128 - 32 * i, 1), 0.0))
        return jnp.concatenate(pieces, axis=0)

    before, _, scale = eliminate(unpack(part_p), count)
    weights = before * scale
    for k in range(total):
        spread[k] = jnp.broadcast_to(weights[:, 32 + k : 33 + k], (32, 128))

    mine, diagonal, my_scale = eliminate(unpack(part_z), count)
    lane = signs((8, 128), 1)
    pivot_row = jnp.broadcast_to(jnp.sum(diagonal, axis=0, keepdims=True), (8, 128))
    logs[seg] = 0.5 * jnp.log(jnp.where(lane < count, pivot_row, 1.0))

    def exchange_log(d):
        return remote(logs.at[seg], logs.at[seg], log_send.at[d], log_recv.at[seg], along_seg(d))

    for d in range(1, n_seg):
        exchange_log(d).start()
    inner = jnp.where(rows == lanes, mine[:, count : count + 1] * my_scale, 0.0)
    proj[...] = jnp.sum(inner, axis=0, keepdims=True)[:, :count]

    for k in range(total):
        shift(k).wait_recv()

    @pl.when(seg == 0)
    def _():
        copy = pltpu.make_async_copy(tang, handed, out_sems.at[0])
        copy.start()
        copy.wait()

    @pl.when(seg > 0)
    def _():
        def combine(i, carry):
            c, x = i // SLAB, lax.rem(i, SLAB)
            w = [prev[k, c, x] for k in range(total)]
            for j in range(total):
                new = jnp.broadcast_to(spread[0, j : j + 1, :], (8, 128)) * w[0]
                for k in range(1, j + 1):
                    new += jnp.broadcast_to(spread[k, j : j + 1, :], (8, 128)) * w[k]
                outv[j, c, x] = new
            return carry

        def out(c):
            return pltpu.make_async_copy(outv.at[:, c], handed.at[0, :, c], out_sems.at[c])

        for c in range(3):
            lax.fori_loop(c * SLAB, (c + 1) * SLAB, combine, 0)
            out(c).start()
        for c in range(3):
            out(c).wait()

    for d in range(1, n_seg):
        arrived(logs, log_recv, lax.rem(seg + d, n_seg))
    sums = jnp.zeros((8, 128), jnp.float32)
    for i in range(n_seg):
        sums = sums + jnp.where(i <= seg, logs[i], 0.0)
    growth[...] = sums[0:1, :count]

    for copy in sides:
        copy.wait_send()

    def left_here(k, carry):
        for copy in halo(k):
            copy.wait_send()
        shift(k).wait_send()
        return carry

    lax.fori_loop(0, total, left_here, 0)
    for d in range(1, ROW):
        exchange_y(d).wait_send()
    for d in range(1, depth):
        exchange_z(d).wait_send()
    for d in range(depth):
        exchange_p(d).wait_send()
    for d in range(1, n_seg):
        exchange_log(d).wait_send()


def body(tangents, base_flow, viscosity, source):
    n_seg, n_space = lax.axis_size("seg"), lax.axis_size("space")
    total = tangents.shape[1]
    count = total - 1
    depth = n_space // ROW
    f32 = jnp.float32
    field = (3, SLAB, 8, 128)
    dma = pltpu.SemaphoreType.DMA
    any_spec = pl.BlockSpec(memory_space=pl.ANY)
    vmem_spec = pl.BlockSpec(memory_space=pltpu.VMEM)
    return pl.pallas_call(
        functools.partial(kernel, (n_seg, n_space, count)),
        out_shape=(
            jax.ShapeDtypeStruct(tangents.shape, f32),
            jax.ShapeDtypeStruct((1, count), f32),
            jax.ShapeDtypeStruct((1, count), f32),
        ),
        in_specs=[any_spec] * 4,
        out_specs=(any_spec, vmem_spec, vmem_spec),
        scratch_shapes=[
            pltpu.VMEM((total, 3, WIDE, 8, 128), f32),
            pltpu.VMEM((STEPS, 3, WIDE, 8, 128), f32),
            pltpu.VMEM((WIDE, 8, 128), f32),
            pltpu.VMEM((3, WIDE, 8, 128), f32),
            pltpu.VMEM((STEPS, 15, WIDE, 8, 128), f32),
            pltpu.VMEM((3, WIDE, 8, 128), f32),
            pltpu.VMEM((3, WIDE, 8, 128), f32),
            pltpu.VMEM((total,) + field, f32),
            pltpu.VMEM((total,) + field, f32),
            pltpu.VMEM((total,) + field, f32),
            pltpu.VMEM((256, 128), f32),
            pltpu.VMEM((32, 128), f32),
            pltpu.VMEM((total, 32, 128), f32),
            pltpu.VMEM((ROW, 8, 128), f32),
            pltpu.VMEM((depth, 8, 128), f32),
            pltpu.VMEM((depth, 8, 128), f32),
            pltpu.VMEM((n_seg, 8, 128), f32),
            dma((4,)),
            dma((2, total)),
            dma((2, total)),
            dma((2, 6)),
            dma((2, 6)),
            dma((total,)),
            dma((total,)),
            dma((ROW,)),
            dma((ROW,)),
            dma((depth,)),
            dma((depth,)),
            dma((depth,)),
            dma((depth,)),
            dma((n_seg,)),
            dma((n_seg,)),
            dma((3,)),
        ],
        compiler_params=pltpu.CompilerParams(
            collective_id=0, has_side_effects=True, vmem_limit_bytes=40 * 1024 * 1024
        ),
    )(tangents, base_flow, viscosity, source)


def solution(mesh):
    return jax.shard_map(
        body,
        mesh=mesh,
        in_specs=(
            P("seg", None, None, "space", None, None),
            P("seg", None, None, "space", None, None),
            P("seg", "space", None, None),
            P("seg", None, "space", None, None),
        ),
        out_specs=(P("seg", None, None, "space", None, None), P("seg", None), P("seg", None)),
        check_vma=False,
    )
```

time: 785 us -> 70.9 us (0.09); the launches traced: 777 us -> 70.5 us
  other arithmetic: 384 us -> 0 us
  blocking collectives: 225 us -> 0 us
  Pallas kernels: 0 us -> 64.1 us
  local copies, waits for them, and re-layouts: 51.2 us -> 5.77 us
  starting transfers between devices: 44.9 us -> 0 us
  waiting for transfers between devices: 30.6 us -> 0 us
  matrix products: 22.8 us -> 0 us
  between operations: 18.5 us -> 0.65 us
    select_n x34 -> x0, other arithmetic: 185 us -> none  [the longest x27 184 us: lower_cholesky(): jnp.where(places >= column_index, accum / pivot, jnp.zeros_like(accum))]
    psum x2 -> x0, blocking collectives: 180 us -> none  [the longest x1 124 us: body(): gram_matrix = lax.psum(local_gram, 'space')]
    sub x24 -> x0, other arithmetic: 172 us -> none  [the longest x23 172 us: lower_cholesky(): accum = accum - columns[earlier] * columns[earlier][column_index]]
    pallas_call x0 -> x1, Pallas kernels: none -> 64.1 us  [body(): pl.pallas_call(functools.partial(kernel, (n_seg, n_space, count)), out_sh...]
    unnamed x1 -> x0, blocking collectives: 45.1 us -> none
    ppermute x11 -> x0, starting transfers between devices: 44.9 us -> none  [the longest x5 23.4 us: extended_2(): before = lax.ppermute(last, axis, up)]
    slice x82 -> x0, local copies, waits for them, and re-layouts: 42 us -> none  [the longest x24 14.8 us: lower_cholesky(): pivot = jnp.sqrt(accum[column_index])]
    ppermute x11 -> x0, waiting for transfers between devices: 30.6 us -> none  [the longest x5 14.5 us: extended_2(): after = lax.ppermute(first, axis, down)]
  transfers between devices with their start and end apart: 11 -> 0, of which waited for: 8 -> 0; matrix products, arithmetic and copies ran while one was open for 1% -> 0% of each run, Pallas kernels for 0% -> 0%
where the time goes in v1:
time: 70.9 us; the launch traced here: 70.5 us
  Pallas kernels  64.1 us (90%)
  local copies, waits for them, and re-layouts  5.77 us (8%)
    pallas_call x1, Pallas kernels, body(): pl.pallas_call(functools.partial(kernel, (n_seg, n_space, count)), out_sh...  64.1 us
    unnamed x11, local copies, waits for them, and re-layouts  5.77 us

profile of v1, /device:TPU:1, one launch (start us, length us, event | category | flops | bytes accessed | tf_op | source)
XLA Modules:
  0.0 70.5 jit_solution(11058404981137670536)
XLA Ops:
  0.6 0.0 copy-start
  0.6 1.3 %copy-done = f32[1,25,3,4,8,128]{5,4,3,2,1,0:T(8,128)S(1)} copy-done((f32[1,25,3,4,8,128]{5,4,3,2,1,0:T(8,128)S(1)}, f32[1,25,3,4,8,128]{5,4,3,2,1,0:T(8,128)}, u32[]{:S(2)}) %copy-start) | copy-done | bytes 1228824
  1.9 0.0 copy-start.1
  1.9 0.9 %copy-done.1 = f32[1,4,3,4,8,128]{5,4,3,2,1,0:T(8,128)S(1)} copy-done((f32[1,4,3,4,8,128]{5,4,3,2,1,0:T(8,128)S(1)}, f32[1,4,3,4,8,128]{5,4,3,2,1,0:T(8,128)}, u32[]{:S(2)}) %copy-start.1) | copy-done | bytes 196632
  2.8 0.0 copy-start.2
  2.8 0.8 %copy-done.2 = f32[1,3,4,8,128]{4,3,2,1,0:T(8,128)S(1)} copy-done((f32[1,3,4,8,128]{4,3,2,1,0:T(8,128)S(1)}, f32[1,3,4,8,128]{4,3,2,1,0:T(8,128)}, u32[]{:S(2)}) %copy-start.2) | copy-done | bytes 49176
  3.6 0.0 copy-start.3
  3.6 0.7 %copy-done.3 = f32[1,4,8,128]{3,2,1,0:T(8,128)S(1)} copy-done((f32[1,4,8,128]{3,2,1,0:T(8,128)S(1)}, f32[1,4,8,128]{3,2,1,0:T(8,128)}, u32[]{:S(2)}) %copy-start.3) | copy-done | bytes 16408
  4.4 64.1 %shard_map.67 = (f32[1,25,3,4,8,128]{5,4,3,2,1,0:T(8,128)S(1)}, f32[1,24]{1,0:T(1,128)S(1)}, f32[1,24]{1,0:T(1,128)S(1)}) custom-call(f32[1,25,3,4,8,128]{5,4,3,2,1,0:T(8,128)S(1)} %copy-done, f32[1,4,3,4,8,128]{5,4,3,2,1,0:T(8,128)S(1)} %copy-done.1, f32[1,4,8,128]{3,2,1,0:T(8,128)S(1)} %copy-done.3, f32[1,3,4,8,128]{4,3,2,1,0:T(8,128)S(1)} %copy-done.2), custom_call_target="tpu_custom_call" | custom-call | tf_op jit(solution)/shard_map/pallas_call | solution.py:349
  68.5 1.0 %copy.10 = f32[1,25,3,4,8,128]{5,4,3,2,1,0:T(8,128)} copy(f32[1,25,3,4,8,128]{5,4,3,2,1,0:T(8,128)S(1)} %get-tuple-element.6) | data formatting | bytes 2457600
  69.5 0.5 copy.11
  70.0 0.5 copy.12
Async XLA Ops:
  0.6 1.3 %copy-start = (f32[1,25,3,4,8,128]{5,4,3,2,1,0:T(8,128)S(1)}, f32[1,25,3,4,8,128]{5,4,3,2,1,0:T(8,128)}, u32[]{:S(2)}) copy-start(f32[1,25,3,4,8,128]{5,4,3,2,1,0:T(8,128)} %tang.1) | copy-start | bytes 3686404
  1.9 0.9 %copy-start.1 = (f32[1,4,3,4,8,128]{5,4,3,2,1,0:T(8,128)S(1)}, f32[1,4,3,4,8,128]{5,4,3,2,1,0:T(8,128)}, u32[]{:S(2)}) copy-start(f32[1,4,3,4,8,128]{5,4,3,2,1,0:T(8,128)} %flow.1) | copy-start | bytes 589828
  2.8 0.8 %copy-start.2 = (f32[1,3,4,8,128]{4,3,2,1,0:T(8,128)S(1)}, f32[1,3,4,8,128]{4,3,2,1,0:T(8,128)}, u32[]{:S(2)}) copy-start(f32[1,3,4,8,128]{4,3,2,1,0:T(8,128)} %src.1) | copy-start | bytes 147460
  3.6 0.7 %copy-start.3 = (f32[1,4,8,128]{3,2,1,0:T(8,128)S(1)}, f32[1,4,8,128]{3,2,1,0:T(8,128)}, u32[]{:S(2)}) copy-start(f32[1,4,8,128]{3,2,1,0:T(8,128)} %visc.1) | copy-start | bytes 49156

commit v2 on v1

--- a/solution.py
+++ b/solution.py
@@ -13,7 +13,7 @@
 SLAB = 4
 WIDE = 3 * SLAB
 STEPS = 4
-AHEAD = 4
+AHEAD = 8
 
 
 def signs(shape, dim):
@@ -86,11 +86,11 @@
     sizes,
     tang, flow, visc, src,
     handed, growth, proj,
-    ext, flowx, viscx, srcx, coef, tmp_a, tmp_b, stepped, prev, outv,
-    accs, gram, spread, part_y, part_z, part_p, logs,
+    ext, flowx, viscx, srcx, coef, tmp_a, tmp_b, stepped, prev,
+    accs, gram, spread, weights, received, part_y, part_z, logs,
     local_sems, halo_send, halo_recv, side_send, side_recv,
-    shift_send, shift_recv, y_send, y_recv, z_send, z_recv, p_send, p_recv,
-    log_send, log_recv, out_sems,
+    shift_send, shift_recv, y_send, y_recv, z_send, z_recv,
+    log_send, log_recv, weight_sems, rounds,
 ):
     n_seg, n_space, count = sizes
     total = count + 1
@@ -109,14 +109,16 @@
     def along_seg(d):
         return (lax.rem(seg + d, n_seg), pos)
 
-    senders = [left, right]
-    senders += [along_y(d) for d in range(1, ROW)]
-    senders += [along_z(d) for d in range(1, depth)]
-    senders += [along_z(d, n_seg - 1) for d in range(1, depth)]
-    senders += [along_seg(d) for d in range(1, n_seg)]
+    near = [along_y(1), along_y(ROW - 1), along_z(1), along_z(depth - 1)]
+    near += [along_seg(d % n_seg) for d in (1, -1, 2, -2)]
+    greeted = [right, left] + near
+
+    def greet(sem, devices):
+        for device in devices:
+            pl.semaphore_signal(sem, inc=1, device_id=device, device_id_type=MESH)
+
     barrier = pltpu.get_barrier_semaphore()
-    for device in senders:
-        pl.semaphore_signal(barrier, inc=1, device_id=device, device_id_type=MESH)
+    greet(barrier, greeted)
 
     own = pl.ds(SLAB, SLAB)
     locals_ = [
@@ -161,12 +163,13 @@
     sides.append(remote(src.at[0, :, pl.ds(0, n)], srcx.at[:, pl.ds(2 * SLAB, n)],
                         side_send.at[1, 5], side_recv.at[1, 5], left))
 
-    pl.semaphore_wait(barrier, len(senders))
+    pl.semaphore_wait(barrier, len(greeted))
     for copy in sides:
         copy.start()
-    for k in range(AHEAD):
+    for k in range(min(AHEAD, total)):
         for copy in halo(k):
             copy.start()
+    greet(rounds.at[0], near)
     for copy in locals_:
         copy.wait()
     for copy in sides:
@@ -187,6 +190,20 @@
         def _():
             for copy in halo(k + AHEAD):
                 copy.start()
+
+        @pl.when(k == 2)
+        def _():
+            pl.semaphore_wait(rounds.at[0], len(near))
+            greet(rounds.at[1], near[2:4])
+
+        @pl.when(k == 4)
+        def _():
+            pl.semaphore_wait(rounds.at[1], 2)
+            greet(rounds.at[2], near[2:4])
+
+        @pl.when(k == 6)
+        def _():
+            pl.semaphore_wait(rounds.at[2], 2)
 
         chain = [ext.at[k], tmp_a, tmp_b, tmp_a, stepped.at[k]]
         for s in range(STEPS):
@@ -231,9 +248,6 @@
     def exchange_z(d):
         return remote(part_z.at[z], part_z.at[z], z_send.at[d], z_recv.at[z], along_z(d))
 
-    def exchange_p(d):
-        return remote(part_z.at[z], part_p.at[z], p_send.at[d], p_recv.at[z], along_z(d, 1))
-
     def arrived(slot, sems, position):
         remote(slot.at[position], slot.at[position], y_send.at[0], sems.at[position], left).wait_recv()
 
@@ -244,12 +258,8 @@
     part_z[z] = part_y[0] + part_y[1] + part_y[2] + part_y[3]
     for d in range(1, depth):
         exchange_z(d).start()
-    for d in range(depth):
-        exchange_p(d).start()
     for d in range(1, depth):
         arrived(part_z, z_recv, lax.rem(z + d, depth))
-    for d in range(depth):
-        arrived(part_p, p_recv, lax.rem(z + d, depth))
 
     def unpack(slots):
         sums = slots[0]
@@ -261,12 +271,10 @@
             pieces.append(jnp.where(narrow, pltpu.roll(sums, 128 - 32 * i, 1), 0.0))
         return jnp.concatenate(pieces, axis=0)
 
-    before, _, scale = eliminate(unpack(part_p), count)
-    weights = before * scale
-    for k in range(total):
-        spread[k] = jnp.broadcast_to(weights[:, 32 + k : 33 + k], (32, 128))
-
-    mine, diagonal, my_scale = eliminate(unpack(part_z), count)
+    mine, diagonal, scale = eliminate(unpack(part_z), count)
+    weights[...] = mine * scale
+    hand_on = remote(weights, received, weight_sems.at[0], weight_sems.at[1], along_seg(1))
+    hand_on.start()
     lane = signs((8, 128), 1)
     pivot_row = jnp.broadcast_to(jnp.sum(diagonal, axis=0, keepdims=True), (8, 128))
     logs[seg] = 0.5 * jnp.log(jnp.where(lane < count, pivot_row, 1.0))
@@ -276,20 +284,26 @@
 
     for d in range(1, n_seg):
         exchange_log(d).start()
-    inner = jnp.where(rows == lanes, mine[:, count : count + 1] * my_scale, 0.0)
+    inner = jnp.where(rows == lanes, mine[:, count : count + 1] * scale, 0.0)
     proj[...] = jnp.sum(inner, axis=0, keepdims=True)[:, :count]
 
     for k in range(total):
         shift(k).wait_recv()
+    hand_on.wait_recv()
 
     @pl.when(seg == 0)
     def _():
-        copy = pltpu.make_async_copy(tang, handed, out_sems.at[0])
-        copy.start()
-        copy.wait()
+        def keep(k, carry):
+            handed[k] = ext[k, :, SLAB : 2 * SLAB]
+            return carry
+
+        lax.fori_loop(0, total, keep, 0)
 
     @pl.when(seg > 0)
     def _():
+        for k in range(total):
+            spread[k] = jnp.broadcast_to(received[:, 32 + k : 33 + k], (32, 128))
+
         def combine(i, carry):
             c, x = i // SLAB, lax.rem(i, SLAB)
             w = [prev[k, c, x] for k in range(total)]
@@ -297,17 +311,10 @@
                 new = jnp.broadcast_to(spread[0, j : j + 1, :], (8, 128)) * w[0]
                 for k in range(1, j + 1):
                     new += jnp.broadcast_to(spread[k, j : j + 1, :], (8, 128)) * w[k]
-                outv[j, c, x] = new
+                handed[j, c, x] = new
             return carry
 
-        def out(c):
-            return pltpu.make_async_copy(outv.at[:, c], handed.at[0, :, c], out_sems.at[c])
-
-        for c in range(3):
-            lax.fori_loop(c * SLAB, (c + 1) * SLAB, combine, 0)
-            out(c).start()
-        for c in range(3):
-            out(c).wait()
+        lax.fori_loop(0, 3 * SLAB, combine, 0)
 
     for d in range(1, n_seg):
         arrived(logs, log_recv, lax.rem(seg + d, n_seg))
@@ -330,10 +337,9 @@
         exchange_y(d).wait_send()
     for d in range(1, depth):
         exchange_z(d).wait_send()
-    for d in range(depth):
-        exchange_p(d).wait_send()
     for d in range(1, n_seg):
         exchange_log(d).wait_send()
+    hand_on.wait_send()
 
 
 def body(tangents, base_flow, viscosity, source):
@@ -346,15 +352,19 @@
     dma = pltpu.SemaphoreType.DMA
     any_spec = pl.BlockSpec(memory_space=pl.ANY)
     vmem_spec = pl.BlockSpec(memory_space=pltpu.VMEM)
-    return pl.pallas_call(
+    inputs = [
+        pltpu.with_memory_space_constraint(x, pltpu.HBM)
+        for x in (tangents, base_flow, viscosity, source)
+    ]
+    handed, growth, proj = pl.pallas_call(
         functools.partial(kernel, (n_seg, n_space, count)),
         out_shape=(
-            jax.ShapeDtypeStruct(tangents.shape, f32),
+            jax.ShapeDtypeStruct((total,) + field, f32),
             jax.ShapeDtypeStruct((1, count), f32),
             jax.ShapeDtypeStruct((1, count), f32),
         ),
         in_specs=[any_spec] * 4,
-        out_specs=(any_spec, vmem_spec, vmem_spec),
+        out_specs=(vmem_spec,) * 3,
         scratch_shapes=[
             pltpu.VMEM((total, 3, WIDE, 8, 128), f32),
             pltpu.VMEM((STEPS, 3, WIDE, 8, 128), f32),
@@ -365,12 +375,12 @@
             pltpu.VMEM((3, WIDE, 8, 128), f32),
             pltpu.VMEM((total,) + field, f32),
             pltpu.VMEM((total,) + field, f32),
-            pltpu.VMEM((total,) + field, f32),
             pltpu.VMEM((256, 128), f32),
             pltpu.VMEM((32, 128), f32),
             pltpu.VMEM((total, 32, 128), f32),
+            pltpu.VMEM((32, 128), f32),
+            pltpu.VMEM((32, 128), f32),
             pltpu.VMEM((ROW, 8, 128), f32),
-            pltpu.VMEM((depth, 8, 128), f32),
             pltpu.VMEM((depth, 8, 128), f32),
             pltpu.VMEM((n_seg, 8, 128), f32),
             dma((4,)),
@@ -384,16 +394,16 @@
             dma((ROW,)),
             dma((depth,)),
             dma((depth,)),
-            dma((depth,)),
-            dma((depth,)),
             dma((n_seg,)),
             dma((n_seg,)),
-            dma((3,)),
+            dma((2,)),
+            pltpu.SemaphoreType.REGULAR((3,)),
         ],
         compiler_params=pltpu.CompilerParams(
-            collective_id=0, has_side_effects=True, vmem_limit_bytes=40 * 1024 * 1024
+            collective_id=0, has_side_effects=True, vmem_limit_bytes=32 * 1024 * 1024
         ),
-    )(tangents, base_flow, viscosity, source)
+    )(*inputs)
+    return (handed[None], growth, proj)
 
 
 def solution(mesh):

time: 70.9 us -> 62.5 us (0.88)
  Pallas kernels: 64.1 us -> 59.7 us
  local copies, waits for them, and re-layouts: 5.77 us -> 2.05 us
    pallas_call x1, Pallas kernels: 64.1 us -> 59.7 us  [body(): pl.pallas_call(functools.partial(kernel, (n_seg, n_space, count)), out_sh...]
    unnamed x11 -> x3, local copies, waits for them, and re-layouts: 5.77 us -> 2.05 us
where the time goes in v2:
time: 62.5 us; the launch traced here: 62.4 us
  Pallas kernels  59.7 us (96%)
  local copies, waits for them, and re-layouts  2.05 us (3%)
  between operations  0.64 us (1%)
    pallas_call x1, Pallas kernels, body(): pl.pallas_call(functools.partial(kernel, (n_seg, n_space, count)), out_sh...  59.7 us
    unnamed x3, local copies, waits for them, and re-layouts  2.05 us

profile of v2, /device:TPU:1, one launch (start us, length us, event | category | flops | bytes accessed | tf_op | source)
XLA Modules:
  0.0 62.4 jit_solution(4982869388867257337)
XLA Ops:
  0.6 59.7 %shard_map.67 = (f32[25,3,4,8,128]{4,3,2,1,0:T(8,128)S(1)}, f32[1,24]{1,0:T(1,128)S(1)}, f32[1,24]{1,0:T(1,128)S(1)}) custom-call(f32[1,25,3,4,8,128]{5,4,3,2,1,0:T(8,128)} %tang.1, f32[1,4,3,4,8,128]{5,4,3,2,1,0:T(8,128)} %flow.1, f32[1,4,8,128]{3,2,1,0:T(8,128)} %visc.1, f32[1,3,4,8,128]{4,3,2,1,0:T(8,128)} %src.1), custom_call_target="tpu_custom_call" | custom-call | tf_op jit(solution)/shard_map/pallas_call | solution.py:359
  60.4 1.0 %copy.10 = f32[1,25,3,4,8,128]{5,4,3,2,1,0:T(8,128)} copy(f32[1,25,3,4,8,128]{5,4,3,2,1,0:T(8,128)S(1)} %bitcast.1) | data formatting | bytes 2457600
  61.4 0.5 copy.11
  61.9 0.5 copy.12

commit v3 on v2

--- a/solution.py
+++ b/solution.py
@@ -11,19 +11,26 @@
 DT = 0.5
 ROW = 4
 SLAB = 4
-WIDE = 3 * SLAB
+HALO = 2
+WIDE = SLAB + 2 * HALO
 STEPS = 4
-AHEAD = 8
+AHEAD = 12
+LAG = 12
 
 
 def signs(shape, dim):
     return lax.broadcasted_iota(jnp.int32, shape, dim)
 
 
+def span(s):
+    edge = 1 + s % HALO
+    return edge, WIDE - edge
+
+
 def coefficients(s, flowx, viscx, srcx, coef, position, planes_total):
-    lo, hi = s + 1, WIDE - 1 - s
+    lo, hi = span(s)
     n = hi - lo
-    first = position * SLAB - SLAB
+    first = position * SLAB - HALO
     plane = first + lo - 1 + signs((n + 2, 8, 128), 0)
     inside = (plane >= 0) & (plane < planes_total)
     ahead_in, behind_in = inside[2:], inside[:n]
@@ -57,7 +64,7 @@
 
 
 def step(s, src, dst, coef, base):
-    lo, hi = s + 1, WIDE - 1 - s
+    lo, hi = span(s)
     w = [src[c, lo:hi] for c in range(3)]
     k = [coef[s, i, lo:hi] for i in range(6)]
     for c in range(3):
@@ -85,12 +92,12 @@
 def kernel(
     sizes,
     tang, flow, visc, src,
-    handed, growth, proj,
-    ext, flowx, viscx, srcx, coef, tmp_a, tmp_b, stepped, prev,
-    accs, gram, spread, weights, received, part_y, part_z, logs,
+    handed, small,
+    ext, mid, flowx, viscx, srcx, coef, tmp_a, tmp_b, stepped, prev,
+    accs, gram, spread, part_y, part_z, part_p, logs,
     local_sems, halo_send, halo_recv, side_send, side_recv,
-    shift_send, shift_recv, y_send, y_recv, z_send, z_recv,
-    log_send, log_recv, weight_sems, rounds,
+    shift_send, shift_recv, y_send, y_recv, z_send, z_recv, p_send, p_recv,
+    log_send, log_recv, rounds,
 ):
     n_seg, n_space, count = sizes
     total = count + 1
@@ -120,7 +127,7 @@
     barrier = pltpu.get_barrier_semaphore()
     greet(barrier, greeted)
 
-    own = pl.ds(SLAB, SLAB)
+    own = pl.ds(HALO, SLAB)
     locals_ = [
         pltpu.make_async_copy(tang.at[0], ext.at[:, :, own], local_sems.at[0]),
         pltpu.make_async_copy(flow.at[0], flowx.at[:, :, own], local_sems.at[1]),
@@ -140,27 +147,35 @@
 
     def halo(k):
         return [
-            remote(tang.at[0, k], ext.at[k, :, pl.ds(0, SLAB)],
+            remote(tang.at[0, k, :, pl.ds(SLAB - HALO, HALO)], ext.at[k, :, pl.ds(0, HALO)],
                    halo_send.at[0, k], halo_recv.at[0, k], right),
-            remote(tang.at[0, k], ext.at[k, :, pl.ds(2 * SLAB, SLAB)],
+            remote(tang.at[0, k, :, pl.ds(0, HALO)], ext.at[k, :, pl.ds(SLAB + HALO, HALO)],
                    halo_send.at[1, k], halo_recv.at[1, k], left),
         ]
 
+    def second(k):
+        return [
+            remote(mid.at[k, :, pl.ds(SLAB, HALO)], mid.at[k, :, pl.ds(0, HALO)],
+                   halo_send.at[2, k], halo_recv.at[2, k], right),
+            remote(mid.at[k, :, pl.ds(HALO, HALO)], mid.at[k, :, pl.ds(SLAB + HALO, HALO)],
+                   halo_send.at[3, k], halo_recv.at[3, k], left),
+        ]
+
     sides = []
     for s in range(STEPS):
-        n = SLAB - s
-        sides.append(remote(flow.at[0, s, :, pl.ds(s, n)], flowx.at[s, :, pl.ds(s, n)],
+        n = HALO - s % HALO
+        sides.append(remote(flow.at[0, s, :, pl.ds(SLAB - n, n)], flowx.at[s, :, pl.ds(HALO - n, n)],
                             side_send.at[0, s], side_recv.at[0, s], right))
-        sides.append(remote(flow.at[0, s, :, pl.ds(0, n)], flowx.at[s, :, pl.ds(2 * SLAB, n)],
+        sides.append(remote(flow.at[0, s, :, pl.ds(0, n)], flowx.at[s, :, pl.ds(SLAB + HALO, n)],
                             side_send.at[1, s], side_recv.at[1, s], left))
-    n = SLAB - 1
-    sides.append(remote(visc.at[0, pl.ds(1, n)], viscx.at[pl.ds(1, n)],
+    n = HALO - 1
+    sides.append(remote(visc.at[0, pl.ds(SLAB - n, n)], viscx.at[pl.ds(HALO - n, n)],
                         side_send.at[0, 4], side_recv.at[0, 4], right))
-    sides.append(remote(visc.at[0, pl.ds(0, n)], viscx.at[pl.ds(2 * SLAB, n)],
+    sides.append(remote(visc.at[0, pl.ds(0, n)], viscx.at[pl.ds(SLAB + HALO, n)],
                         side_send.at[1, 4], side_recv.at[1, 4], left))
-    sides.append(remote(src.at[0, :, pl.ds(1, n)], srcx.at[:, pl.ds(1, n)],
+    sides.append(remote(src.at[0, :, pl.ds(SLAB - n, n)], srcx.at[:, pl.ds(HALO - n, n)],
                         side_send.at[0, 5], side_recv.at[0, 5], right))
-    sides.append(remote(src.at[0, :, pl.ds(0, n)], srcx.at[:, pl.ds(2 * SLAB, n)],
+    sides.append(remote(src.at[0, :, pl.ds(0, n)], srcx.at[:, pl.ds(SLAB + HALO, n)],
                         side_send.at[1, 5], side_recv.at[1, 5], left))
 
     pl.semaphore_wait(barrier, len(greeted))
@@ -182,7 +197,17 @@
 
     rows, lanes = signs((32, 128), 0), signs((32, 128), 1)
 
-    def one(k, carry):
+    def advance(k, s, src, dst, base):
+        step(s, src, dst, coef, base)
+
+        @pl.when(k == count)
+        def _():
+            lo, hi = span(s)
+            for c in range(3):
+                driven = dst[c, lo - base : hi - base]
+                dst[c, lo - base : hi - base] = driven + DT * srcx[c, lo:hi]
+
+    def start(k):
         for copy in halo(k):
             copy.wait_recv()
 
@@ -191,33 +216,16 @@
             for copy in halo(k + AHEAD):
                 copy.start()
 
-        @pl.when(k == 2)
-        def _():
-            pl.semaphore_wait(rounds.at[0], len(near))
-            greet(rounds.at[1], near[2:4])
-
-        @pl.when(k == 4)
-        def _():
-            pl.semaphore_wait(rounds.at[1], 2)
-            greet(rounds.at[2], near[2:4])
-
-        @pl.when(k == 6)
-        def _():
-            pl.semaphore_wait(rounds.at[2], 2)
-
-        chain = [ext.at[k], tmp_a, tmp_b, tmp_a, stepped.at[k]]
-        for s in range(STEPS):
-            final = s == STEPS - 1
-            step(s, chain[s], chain[s + 1], coef, SLAB if final else 0)
-
-            @pl.when(k == count)
-            def _():
-                lo, hi = s + 1, WIDE - 1 - s
-                base = SLAB if final else 0
-                dst = chain[s + 1]
-                for c in range(3):
-                    dst[c, lo - base : hi - base] = dst[c, lo - base : hi - base] + DT * srcx[c, lo:hi]
-
+        advance(k, 0, ext.at[k], tmp_a, 0)
+        advance(k, 1, tmp_a, mid.at[k], 0)
+        for copy in second(k):
+            copy.start()
+
+    def finish(k):
+        for copy in second(k):
+            copy.wait_recv()
+        advance(k, 2, mid.at[k], tmp_b, 0)
+        advance(k, 3, tmp_b, stepped.at[k], HALO)
         shift(k).start()
         w = stepped[k]
         for j in range(total):
@@ -231,10 +239,40 @@
         g = jnp.where((lanes == k) & (rows <= k), column, g)
         g = jnp.where((rows == k) & (lanes <= k), row, g)
         gram[...] = g
+
+    def turn(i, carry):
+        @pl.when(i == 2)
+        def _():
+            pl.semaphore_wait(rounds.at[0], len(near))
+            greet(rounds.at[1], near[2:4])
+
+        @pl.when(i == 4)
+        def _():
+            pl.semaphore_wait(rounds.at[1], 2)
+            greet(rounds.at[2], near[2:4])
+
+        @pl.when(i == 6)
+        def _():
+            pl.semaphore_wait(rounds.at[2], 2)
+            greet(rounds.at[3], near[2:4])
+
+        @pl.when(i == 8)
+        def _():
+            pl.semaphore_wait(rounds.at[3], 2)
+
+        @pl.when(i < total)
+        def _():
+            start(i)
+
+        @pl.when(i >= lag)
+        def _():
+            finish(i - lag)
+
         return carry
 
+    lag = min(LAG, total)
     accs[8 * total :, :] = jnp.zeros((8 * (32 - total), 128), jnp.float32)
-    lax.fori_loop(0, total, one, 0)
+    lax.fori_loop(0, total + lag, turn, 0)
 
     cells = 3 * SLAB * 8 * 128 * n_space
     packed = gram[0:8, :]
@@ -248,6 +286,9 @@
     def exchange_z(d):
         return remote(part_z.at[z], part_z.at[z], z_send.at[d], z_recv.at[z], along_z(d))
 
+    def exchange_p(d):
+        return remote(part_z.at[z], part_p.at[z], p_send.at[d], p_recv.at[z], along_z(d, 1))
+
     def arrived(slot, sems, position):
         remote(slot.at[position], slot.at[position], y_send.at[0], sems.at[position], left).wait_recv()
 
@@ -256,8 +297,23 @@
     for d in range(1, ROW):
         arrived(part_y, y_recv, lax.rem(y + d, ROW))
     part_z[z] = part_y[0] + part_y[1] + part_y[2] + part_y[3]
-    for d in range(1, depth):
+    far_first = sorted(range(depth), key=lambda d: -min(d, depth - d))
+    for d in far_first[:-1]:
         exchange_z(d).start()
+    for d in far_first:
+        exchange_p(d).start()
+
+    def settle(k, carry):
+        for copy in halo(k) + second(k):
+            copy.wait_send()
+        shift(k).wait()
+        return carry
+
+    for copy in sides:
+        copy.wait_send()
+    lax.fori_loop(0, total, settle, 0)
+    for d in range(1, ROW):
+        exchange_y(d).wait_send()
     for d in range(1, depth):
         arrived(part_z, z_recv, lax.rem(z + d, depth))
 
@@ -272,9 +328,6 @@
         return jnp.concatenate(pieces, axis=0)
 
     mine, diagonal, scale = eliminate(unpack(part_z), count)
-    weights[...] = mine * scale
-    hand_on = remote(weights, received, weight_sems.at[0], weight_sems.at[1], along_seg(1))
-    hand_on.start()
     lane = signs((8, 128), 1)
     pivot_row = jnp.broadcast_to(jnp.sum(diagonal, axis=0, keepdims=True), (8, 128))
     logs[seg] = 0.5 * jnp.log(jnp.where(lane < count, pivot_row, 1.0))
@@ -282,27 +335,30 @@
     def exchange_log(d):
         return remote(logs.at[seg], logs.at[seg], log_send.at[d], log_recv.at[seg], along_seg(d))
 
-    for d in range(1, n_seg):
+    for d in sorted(range(1, n_seg), key=lambda d: -min(d, n_seg - d)):
         exchange_log(d).start()
+    for d in range(1, depth):
+        exchange_z(d).wait_send()
+    for d in range(depth):
+        arrived(part_p, p_recv, lax.rem(z + d, depth))
     inner = jnp.where(rows == lanes, mine[:, count : count + 1] * scale, 0.0)
-    proj[...] = jnp.sum(inner, axis=0, keepdims=True)[:, :count]
-
-    for k in range(total):
-        shift(k).wait_recv()
-    hand_on.wait_recv()
+    small[1:2, :] = jnp.sum(inner, axis=0, keepdims=True)
+
 
     @pl.when(seg == 0)
     def _():
         def keep(k, carry):
-            handed[k] = ext[k, :, SLAB : 2 * SLAB]
+            handed[k] = ext[k, :, HALO : HALO + SLAB]
             return carry
 
         lax.fori_loop(0, total, keep, 0)
 
     @pl.when(seg > 0)
     def _():
+        before, _, before_scale = eliminate(unpack(part_p), count)
+        weights = before * before_scale
         for k in range(total):
-            spread[k] = jnp.broadcast_to(received[:, 32 + k : 33 + k], (32, 128))
+            spread[k] = jnp.broadcast_to(weights[:, 32 + k : 33 + k], (32, 128))
 
         def combine(i, carry):
             c, x = i // SLAB, lax.rem(i, SLAB)
@@ -321,25 +377,12 @@
     sums = jnp.zeros((8, 128), jnp.float32)
     for i in range(n_seg):
         sums = sums + jnp.where(i <= seg, logs[i], 0.0)
-    growth[...] = sums[0:1, :count]
-
-    for copy in sides:
-        copy.wait_send()
-
-    def left_here(k, carry):
-        for copy in halo(k):
-            copy.wait_send()
-        shift(k).wait_send()
-        return carry
-
-    lax.fori_loop(0, total, left_here, 0)
-    for d in range(1, ROW):
-        exchange_y(d).wait_send()
-    for d in range(1, depth):
-        exchange_z(d).wait_send()
+    small[0:1, :] = sums[0:1, :]
+
+    for d in range(depth):
+        exchange_p(d).wait_send()
     for d in range(1, n_seg):
         exchange_log(d).wait_send()
-    hand_on.wait_send()
 
 
 def body(tangents, base_flow, viscosity, source):
@@ -356,16 +399,16 @@
         pltpu.with_memory_space_constraint(x, pltpu.HBM)
         for x in (tangents, base_flow, viscosity, source)
     ]
-    handed, growth, proj = pl.pallas_call(
+    handed, small = pl.pallas_call(
         functools.partial(kernel, (n_seg, n_space, count)),
         out_shape=(
             jax.ShapeDtypeStruct((total,) + field, f32),
-            jax.ShapeDtypeStruct((1, count), f32),
-            jax.ShapeDtypeStruct((1, count), f32),
+            jax.ShapeDtypeStruct((8, 128), f32),
         ),
         in_specs=[any_spec] * 4,
-        out_specs=(vmem_spec,) * 3,
+        out_specs=(vmem_spec,) * 2,
         scratch_shapes=[
+            pltpu.VMEM((total, 3, WIDE, 8, 128), f32),
             pltpu.VMEM((total, 3, WIDE, 8, 128), f32),
             pltpu.VMEM((STEPS, 3, WIDE, 8, 128), f32),
             pltpu.VMEM((WIDE, 8, 128), f32),
@@ -378,14 +421,13 @@
             pltpu.VMEM((256, 128), f32),
             pltpu.VMEM((32, 128), f32),
             pltpu.VMEM((total, 32, 128), f32),
-            pltpu.VMEM((32, 128), f32),
-            pltpu.VMEM((32, 128), f32),
             pltpu.VMEM((ROW, 8, 128), f32),
+            pltpu.VMEM((depth, 8, 128), f32),
             pltpu.VMEM((depth, 8, 128), f32),
             pltpu.VMEM((n_seg, 8, 128), f32),
             dma((4,)),
-            dma((2, total)),
-            dma((2, total)),
+            dma((4, total)),
+            dma((4, total)),
             dma((2, 6)),
             dma((2, 6)),
             dma((total,)),
@@ -394,16 +436,17 @@
             dma((ROW,)),
             dma((depth,)),
             dma((depth,)),
+            dma((depth,)),
+            dma((depth,)),
             dma((n_seg,)),
             dma((n_seg,)),
-            dma((2,)),
-            pltpu.SemaphoreType.REGULAR((3,)),
+            pltpu.SemaphoreType.REGULAR((4,)),
         ],
         compiler_params=pltpu.CompilerParams(
             collective_id=0, has_side_effects=True, vmem_limit_bytes=32 * 1024 * 1024
         ),
     )(*inputs)
-    return (handed[None], growth, proj)
+    return (handed[None], small[0:1, :count], small[1:2, :count])
 
 
 def solution(mesh):

time: 62.5 us -> 60.8 us (0.973)
  Pallas kernels: 59.7 us -> 58.6 us
    pallas_call x1, Pallas kernels: 59.7 us -> 58.6 us  [body(): pl.pallas_call(functools.partial(kernel, (n_seg, n_space, count)), out_sh...]
    unnamed x3 -> x1, local copies, waits for them, and re-layouts: 2.05 us -> 1.03 us
where the time goes in v3:
time: 60.8 us; the launch traced here: 60.7 us
  Pallas kernels  58.6 us (96%)
  local copies, waits for them, and re-layouts  1.55 us (3%)
  between operations  0.64 us (1%)
    pallas_call x1, Pallas kernels, body(): pl.pallas_call(functools.partial(kernel, (n_seg, n_space, count)), out_sh...  58.6 us

profile of v3, /device:TPU:1, one launch (start us, length us, event | category | flops | bytes accessed | tf_op | source)
XLA Modules:
  0.0 60.7 jit_solution(7126349133543495761)
XLA Ops:
  0.6 58.6 %shard_map.67 = (f32[25,3,4,8,128]{4,3,2,1,0:T(8,128)S(1)}, f32[8,128]{1,0:T(8,128)S(1)}) custom-call(f32[1,25,3,4,8,128]{5,4,3,2,1,0:T(8,128)} %tang.1, f32[1,4,3,4,8,128]{5,4,3,2,1,0:T(8,128)} %flow.1, f32[1,4,8,128]{3,2,1,0:T(8,128)} %visc.1, f32[1,3,4,8,128]{4,3,2,1,0:T(8,128)} %src.1), custom_call_target="tpu_custom_call" | custom-call | tf_op jit(solution)/shard_map/pallas_call | solution.py:402
  59.2 0.5 fusion
  59.7 1.0 %copy.8 = f32[1,25,3,4,8,128]{5,4,3,2,1,0:T(8,128)} copy(f32[1,25,3,4,8,128]{5,4,3,2,1,0:T(8,128)S(1)} %bitcast.1) | data formatting | bytes 2457600

commit v4 on v3

--- a/solution.py
+++ b/solution.py
@@ -15,6 +15,7 @@
 WIDE = SLAB + 2 * HALO
 STEPS = 4
 AHEAD = 12
+BEHIND = 6
 LAG = 12
 
 
@@ -92,7 +93,7 @@
 def kernel(
     sizes,
     tang, flow, visc, src,
-    handed, small,
+    handed, growth, proj,
     ext, mid, flowx, viscx, srcx, coef, tmp_a, tmp_b, stepped, prev,
     accs, gram, spread, part_y, part_z, part_p, logs,
     local_sems, halo_send, halo_recv, side_send, side_recv,
@@ -227,6 +228,13 @@
         advance(k, 2, mid.at[k], tmp_b, 0)
         advance(k, 3, tmp_b, stepped.at[k], HALO)
         shift(k).start()
+        for copy in halo(k) + second(k):
+            copy.wait_send()
+
+        @pl.when(k >= BEHIND)
+        def _():
+            shift(k - BEHIND).wait()
+
         w = stepped[k]
         for j in range(total):
             accs[8 * j : 8 * j + 8, :] = jnp.sum(w * stepped[j], axis=(0, 1))
@@ -303,15 +311,10 @@
     for d in far_first:
         exchange_p(d).start()
 
-    def settle(k, carry):
-        for copy in halo(k) + second(k):
-            copy.wait_send()
-        shift(k).wait()
-        return carry
-
     for copy in sides:
         copy.wait_send()
-    lax.fori_loop(0, total, settle, 0)
+    for k in range(max(total - BEHIND, 0), total):
+        shift(k).wait()
     for d in range(1, ROW):
         exchange_y(d).wait_send()
     for d in range(1, depth):
@@ -336,13 +339,17 @@
         return remote(logs.at[seg], logs.at[seg], log_send.at[d], log_recv.at[seg], along_seg(d))
 
     for d in sorted(range(1, n_seg), key=lambda d: -min(d, n_seg - d)):
-        exchange_log(d).start()
+
+        @pl.when(seg + d < n_seg)
+        def _():
+            exchange_log(d).start()
+
     for d in range(1, depth):
         exchange_z(d).wait_send()
     for d in range(depth):
         arrived(part_p, p_recv, lax.rem(z + d, depth))
     inner = jnp.where(rows == lanes, mine[:, count : count + 1] * scale, 0.0)
-    small[1:2, :] = jnp.sum(inner, axis=0, keepdims=True)
+    proj[...] = jnp.sum(inner, axis=0, keepdims=True)[:, :count]
 
 
     @pl.when(seg == 0)
@@ -373,16 +380,43 @@
         lax.fori_loop(0, 3 * SLAB, combine, 0)
 
     for d in range(1, n_seg):
-        arrived(logs, log_recv, lax.rem(seg + d, n_seg))
-    sums = jnp.zeros((8, 128), jnp.float32)
-    for i in range(n_seg):
-        sums = sums + jnp.where(i <= seg, logs[i], 0.0)
-    small[0:1, :] = sums[0:1, :]
+
+        @pl.when(seg >= d)
+        def _():
+            arrived(logs, log_recv, lax.rem(seg + n_seg - d, n_seg))
+
+    sums = tmp_a.at[0, 0]
+    sums[...] = logs[0]
+    for i in range(1, n_seg):
+
+        @pl.when(i <= seg)
+        def _():
+            sums[...] += logs[i]
+
+    growth[...] = sums[0:1, :count]
 
     for d in range(depth):
         exchange_p(d).wait_send()
     for d in range(1, n_seg):
-        exchange_log(d).wait_send()
+
+        @pl.when(seg + d < n_seg)
+        def _():
+            exchange_log(d).wait_send()
+
+
+def deliver(handed_in, growth_in, proj_in, handed, growth, proj, sems):
+    copies = [
+        pltpu.make_async_copy(growth_in, growth, sems.at[0]),
+        pltpu.make_async_copy(proj_in, proj, sems.at[1]),
+    ]
+    total = handed_in.shape[0]
+    for i in range(0, total, 5):
+        part = pl.ds(i, min(5, total - i))
+        copies.append(pltpu.make_async_copy(handed_in.at[part], handed.at[0, part], sems.at[2 + i]))
+    for copy in copies:
+        copy.start()
+    for copy in copies:
+        copy.wait()
 
 
 def body(tangents, base_flow, viscosity, source):
@@ -399,14 +433,15 @@
         pltpu.with_memory_space_constraint(x, pltpu.HBM)
         for x in (tangents, base_flow, viscosity, source)
     ]
-    handed, small = pl.pallas_call(
+    results = pl.pallas_call(
         functools.partial(kernel, (n_seg, n_space, count)),
         out_shape=(
             jax.ShapeDtypeStruct((total,) + field, f32),
-            jax.ShapeDtypeStruct((8, 128), f32),
+            jax.ShapeDtypeStruct((1, count), f32),
+            jax.ShapeDtypeStruct((1, count), f32),
         ),
         in_specs=[any_spec] * 4,
-        out_specs=(vmem_spec,) * 2,
+        out_specs=(vmem_spec,) * 3,
         scratch_shapes=[
             pltpu.VMEM((total, 3, WIDE, 8, 128), f32),
             pltpu.VMEM((total, 3, WIDE, 8, 128), f32),
@@ -446,7 +481,15 @@
             collective_id=0, has_side_effects=True, vmem_limit_bytes=32 * 1024 * 1024
         ),
     )(*inputs)
-    return (handed[None], small[0:1, :count], small[1:2, :count])
+    small = jax.ShapeDtypeStruct((1, count), f32)
+    return pl.pallas_call(
+        deliver,
+        out_shape=(jax.ShapeDtypeStruct(tangents.shape, f32), small, small),
+        in_specs=[any_spec] * 3,
+        out_specs=(any_spec,) * 3,
+        scratch_shapes=[dma((2 + total,))],
+        compiler_params=pltpu.CompilerParams(vmem_limit_bytes=1024 * 1024),
+    )(*results)
 
 
 def solution(mesh):

time: 60.8 us -> 58.7 us (0.965); the launches traced: 60.7 us -> 57.8 us
  local copies, waits for them, and re-layouts: 1.55 us -> 0 us
  Pallas kernels: 58.6 us -> 57.1 us
    pallas_call x1, Pallas kernels: 58.6 us -> 55.9 us  [body(): pl.pallas_call(functools.partial(kernel, (n_seg, n_space, count)), out_sh...]
    pallas_call x0 -> x1, Pallas kernels: none -> 1.27 us  [body(): pl.pallas_call(deliver, out_shape=(jax.ShapeDtypeStruct(tangents.shape, f...]
    unnamed x1 -> x0, local copies, waits for them, and re-layouts: 1.03 us -> none
where the time goes in v4:
time: 58.7 us; the launch traced here: 57.8 us
  Pallas kernels  57.1 us (97%)
  between operations  0.64 us (1%)
    pallas_call x1, Pallas kernels, body(): pl.pallas_call(functools.partial(kernel, (n_seg, n_space, count)), out_sh...  55.9 us
    pallas_call x1, Pallas kernels, body(): pl.pallas_call(deliver, out_shape=(jax.ShapeDtypeStruct(tangents.shape, f...  1.27 us

profile of v4, /device:TPU:1, one launch (start us, length us, event | category | flops | bytes accessed | tf_op | source)
XLA Modules:
  0.0 57.8 jit_solution(9070161342100220226)
XLA Ops:
  0.6 55.9 %shard_map.67 = (f32[25,3,4,8,128]{4,3,2,1,0:T(8,128)S(1)}, f32[1,24]{1,0:T(1,128)S(1)}, f32[1,24]{1,0:T(1,128)S(1)}) custom-call(f32[1,25,3,4,8,128]{5,4,3,2,1,0:T(8,128)} %tang.1, f32[1,4,3,4,8,128]{5,4,3,2,1,0:T(8,128)} %flow.1, f32[1,4,8,128]{3,2,1,0:T(8,128)} %visc.1, f32[1,3,4,8,128]{4,3,2,1,0:T(8,128)} %src.1), custom_call_target="tpu_custom_call" | custom-call | tf_op jit(solution)/shard_map/pallas_call | solution.py:436
  56.5 1.3 %shard_map.68 = (f32[1,25,3,4,8,128]{5,4,3,2,1,0:T(8,128)}, f32[1,24]{1,0:T(1,128)}, f32[1,24]{1,0:T(1,128)}) custom-call(f32[25,3,4,8,128]{4,3,2,1,0:T(8,128)S(1)} %get-tuple-element.6.handed_in, f32[1,24]{1,0:T(1,128)S(1)} %get-tuple-element.7.growth_in, f32[1,24]{1,0:T(1,128)S(1)} %get-tuple-element.8.proj_in), custom_call_target="tpu_custom_call" | custom-call | tf_op jit(solution)/shard_map/pallas_call | solution.py:485

commit v5 on v4

--- a/solution.py
+++ b/solution.py
@@ -16,6 +16,7 @@
 STEPS = 4
 AHEAD = 12
 BEHIND = 6
+BLOCK = 8
 LAG = 12
 
 
@@ -80,10 +81,14 @@
 def eliminate(gram, count):
     rows, lanes = signs((32, 128), 0), signs((32, 128), 1)
     a = jnp.where(lanes == rows + 32, 1.0, gram)
-    for j in range(count):
-        row = a[j : j + 1, :]
-        m = jnp.where(rows > j, a[:, j : j + 1] * (1.0 / a[j : j + 1, j : j + 1]), 0.0)
-        a = a - m * row
+    for first in range(0, count, BLOCK):
+        pivots = range(first, min(first + BLOCK, count))
+        column = {j: jnp.broadcast_to(a[:, j : j + 1], (32, 128)) for j in pivots}
+        for j in pivots:
+            m = jnp.where(rows > j, column[j] * (1.0 / column[j][j : j + 1, :]), 0.0)
+            for later in pivots[j - first + 1 :]:
+                column[later] = column[later] - m * column[later][j : j + 1, :]
+            a = a - m * a[j : j + 1, :]
     diagonal = jnp.where(lanes == rows, a, 0.0)
     pivots = jnp.sum(diagonal, axis=1, keepdims=True)
     scale = jnp.where(rows[:, :1] < count, 1.0 / jnp.sqrt(pivots), 1.0)
@@ -148,9 +153,9 @@
 
     def halo(k):
         return [
-            remote(tang.at[0, k, :, pl.ds(SLAB - HALO, HALO)], ext.at[k, :, pl.ds(0, HALO)],
+            remote(ext.at[k, :, pl.ds(SLAB, HALO)], ext.at[k, :, pl.ds(0, HALO)],
                    halo_send.at[0, k], halo_recv.at[0, k], right),
-            remote(tang.at[0, k, :, pl.ds(0, HALO)], ext.at[k, :, pl.ds(SLAB + HALO, HALO)],
+            remote(ext.at[k, :, pl.ds(HALO, HALO)], ext.at[k, :, pl.ds(SLAB + HALO, HALO)],
                    halo_send.at[1, k], halo_recv.at[1, k], left),
         ]
 
@@ -165,20 +170,22 @@
     sides = []
     for s in range(STEPS):
         n = HALO - s % HALO
-        sides.append(remote(flow.at[0, s, :, pl.ds(SLAB - n, n)], flowx.at[s, :, pl.ds(HALO - n, n)],
+        sides.append(remote(flowx.at[s, :, pl.ds(HALO + SLAB - n, n)], flowx.at[s, :, pl.ds(HALO - n, n)],
                             side_send.at[0, s], side_recv.at[0, s], right))
-        sides.append(remote(flow.at[0, s, :, pl.ds(0, n)], flowx.at[s, :, pl.ds(SLAB + HALO, n)],
+        sides.append(remote(flowx.at[s, :, pl.ds(HALO, n)], flowx.at[s, :, pl.ds(SLAB + HALO, n)],
                             side_send.at[1, s], side_recv.at[1, s], left))
     n = HALO - 1
-    sides.append(remote(visc.at[0, pl.ds(SLAB - n, n)], viscx.at[pl.ds(HALO - n, n)],
+    sides.append(remote(viscx.at[pl.ds(HALO + SLAB - n, n)], viscx.at[pl.ds(HALO - n, n)],
                         side_send.at[0, 4], side_recv.at[0, 4], right))
-    sides.append(remote(visc.at[0, pl.ds(0, n)], viscx.at[pl.ds(SLAB + HALO, n)],
+    sides.append(remote(viscx.at[pl.ds(HALO, n)], viscx.at[pl.ds(SLAB + HALO, n)],
                         side_send.at[1, 4], side_recv.at[1, 4], left))
-    sides.append(remote(src.at[0, :, pl.ds(SLAB - n, n)], srcx.at[:, pl.ds(HALO - n, n)],
+    sides.append(remote(srcx.at[:, pl.ds(HALO + SLAB - n, n)], srcx.at[:, pl.ds(HALO - n, n)],
                         side_send.at[0, 5], side_recv.at[0, 5], right))
-    sides.append(remote(src.at[0, :, pl.ds(0, n)], srcx.at[:, pl.ds(SLAB + HALO, n)],
+    sides.append(remote(srcx.at[:, pl.ds(HALO, n)], srcx.at[:, pl.ds(SLAB + HALO, n)],
                         side_send.at[1, 5], side_recv.at[1, 5], left))
 
+    for copy in locals_:
+        copy.wait()
     pl.semaphore_wait(barrier, len(greeted))
     for copy in sides:
         copy.start()
@@ -186,8 +193,6 @@
         for copy in halo(k):
             copy.start()
     greet(rounds.at[0], near)
-    for copy in locals_:
-        copy.wait()
     for copy in sides:
         copy.wait_recv()
     for s in range(STEPS):

time: 58.7 us -> 56.6 us (0.964)
  Pallas kernels: 57.1 us -> 55.6 us
    pallas_call x1, Pallas kernels: 55.9 us -> 54.3 us  [body(): pl.pallas_call(functools.partial(kernel, (n_seg, n_space, count)), out_sh...]
where the time goes in v5:
time: 56.6 us; the launch traced here: 56.2 us
  Pallas kernels  55.6 us (98%)
  between operations  0.64 us (1%)
    pallas_call x1, Pallas kernels, body(): pl.pallas_call(functools.partial(kernel, (n_seg, n_space, count)), out_sh...  54.3 us
    pallas_call x1, Pallas kernels, body(): pl.pallas_call(deliver, out_shape=(jax.ShapeDtypeStruct(tangents.shape, f...  1.27 us

profile of v5, /device:TPU:1, one launch (start us, length us, event | category | flops | bytes accessed | tf_op | source)
XLA Modules:
  0.0 56.2 jit_solution(9937427476521453100)
XLA Ops:
  0.6 54.3 %shard_map.67 = (f32[25,3,4,8,128]{4,3,2,1,0:T(8,128)S(1)}, f32[1,24]{1,0:T(1,128)S(1)}, f32[1,24]{1,0:T(1,128)S(1)}) custom-call(f32[1,25,3,4,8,128]{5,4,3,2,1,0:T(8,128)} %tang.1, f32[1,4,3,4,8,128]{5,4,3,2,1,0:T(8,128)} %flow.1, f32[1,4,8,128]{3,2,1,0:T(8,128)} %visc.1, f32[1,3,4,8,128]{4,3,2,1,0:T(8,128)} %src.1), custom_call_target="tpu_custom_call" | custom-call | tf_op jit(solution)/shard_map/pallas_call | solution.py:441
  54.9 1.3 %shard_map.68 = (f32[1,25,3,4,8,128]{5,4,3,2,1,0:T(8,128)}, f32[1,24]{1,0:T(1,128)}, f32[1,24]{1,0:T(1,128)}) custom-call(f32[25,3,4,8,128]{4,3,2,1,0:T(8,128)S(1)} %get-tuple-element.6.handed_in, f32[1,24]{1,0:T(1,128)S(1)} %get-tuple-element.7.growth_in, f32[1,24]{1,0:T(1,128)S(1)} %get-tuple-element.8.proj_in), custom_call_target="tpu_custom_call" | custom-call | tf_op jit(solution)/shard_map/pallas_call | solution.py:490

commit v6 on v5

--- a/solution.py
+++ b/solution.py
@@ -15,7 +15,6 @@
 WIDE = SLAB + 2 * HALO
 STEPS = 4
 AHEAD = 12
-BEHIND = 6
 BLOCK = 8
 LAG = 12
 
@@ -102,7 +101,7 @@
     ext, mid, flowx, viscx, srcx, coef, tmp_a, tmp_b, stepped, prev,
     accs, gram, spread, part_y, part_z, part_p, logs,
     local_sems, halo_send, halo_recv, side_send, side_recv,
-    shift_send, shift_recv, y_send, y_recv, z_send, z_recv, p_send, p_recv,
+    shift_sems, y_send, y_recv, z_send, z_recv, p_send, p_recv,
     log_send, log_recv, rounds,
 ):
     n_seg, n_space, count = sizes
@@ -151,20 +150,23 @@
             device_id=device, device_id_type=MESH,
         )
 
+    def tag(k):
+        return k.start if isinstance(k, pl.Slice) else k
+
     def halo(k):
         return [
             remote(ext.at[k, :, pl.ds(SLAB, HALO)], ext.at[k, :, pl.ds(0, HALO)],
-                   halo_send.at[0, k], halo_recv.at[0, k], right),
+                   halo_send.at[0], halo_recv.at[0, tag(k)], right),
             remote(ext.at[k, :, pl.ds(HALO, HALO)], ext.at[k, :, pl.ds(SLAB + HALO, HALO)],
-                   halo_send.at[1, k], halo_recv.at[1, k], left),
+                   halo_send.at[1], halo_recv.at[1, tag(k)], left),
         ]
 
     def second(k):
         return [
             remote(mid.at[k, :, pl.ds(SLAB, HALO)], mid.at[k, :, pl.ds(0, HALO)],
-                   halo_send.at[2, k], halo_recv.at[2, k], right),
+                   halo_send.at[2], halo_recv.at[2, tag(k)], right),
             remote(mid.at[k, :, pl.ds(HALO, HALO)], mid.at[k, :, pl.ds(SLAB + HALO, HALO)],
-                   halo_send.at[3, k], halo_recv.at[3, k], left),
+                   halo_send.at[3], halo_recv.at[3, tag(k)], left),
         ]
 
     sides = []
@@ -199,7 +201,7 @@
         coefficients(s, flowx, viscx, srcx, coef, pos, n_space * SLAB)
 
     def shift(k):
-        return remote(stepped.at[k], prev.at[k], shift_send.at[k], shift_recv.at[k], along_seg(1))
+        return remote(stepped.at[k], prev.at[k], shift_sems.at[0], shift_sems.at[1], along_seg(1))
 
     rows, lanes = signs((32, 128), 0), signs((32, 128), 1)
 
@@ -233,13 +235,6 @@
         advance(k, 2, mid.at[k], tmp_b, 0)
         advance(k, 3, tmp_b, stepped.at[k], HALO)
         shift(k).start()
-        for copy in halo(k) + second(k):
-            copy.wait_send()
-
-        @pl.when(k >= BEHIND)
-        def _():
-            shift(k - BEHIND).wait()
-
         w = stepped[k]
         for j in range(total):
             accs[8 * j : 8 * j + 8, :] = jnp.sum(w * stepped[j], axis=(0, 1))
@@ -318,8 +313,10 @@
 
     for copy in sides:
         copy.wait_send()
-    for k in range(max(total - BEHIND, 0), total):
-        shift(k).wait()
+    every = pl.ds(0, total)
+    for copy in halo(every) + second(every):
+        copy.wait_send()
+    shift(every).wait()
     for d in range(1, ROW):
         exchange_y(d).wait_send()
     for d in range(1, depth):
@@ -417,7 +414,7 @@
     total = handed_in.shape[0]
     for i in range(0, total, 5):
         part = pl.ds(i, min(5, total - i))
-        copies.append(pltpu.make_async_copy(handed_in.at[part], handed.at[0, part], sems.at[2 + i]))
+        copies.append(pltpu.make_async_copy(handed_in.at[part], handed.at[0, part], sems.at[2 + i // 5]))
     for copy in copies:
         copy.start()
     for copy in copies:
@@ -466,12 +463,11 @@
             pltpu.VMEM((depth, 8, 128), f32),
             pltpu.VMEM((n_seg, 8, 128), f32),
             dma((4,)),
-            dma((4, total)),
+            dma((4,)),
             dma((4, total)),
             dma((2, 6)),
             dma((2, 6)),
-            dma((total,)),
-            dma((total,)),
+            dma((2,)),
             dma((ROW,)),
             dma((ROW,)),
             dma((depth,)),
@@ -492,7 +488,7 @@
         out_shape=(jax.ShapeDtypeStruct(tangents.shape, f32), small, small),
         in_specs=[any_spec] * 3,
         out_specs=(any_spec,) * 3,
-        scratch_shapes=[dma((2 + total,))],
+        scratch_shapes=[dma((2 + -(-total // 5),))],
         compiler_params=pltpu.CompilerParams(vmem_limit_bytes=1024 * 1024),
     )(*results)
 

time: 56.6 us -> 55.1 us (0.973)
  Pallas kernels: 55.6 us -> 54.1 us
    pallas_call x1, Pallas kernels: 54.3 us -> 53 us  [body(): pl.pallas_call(functools.partial(kernel, (n_seg, n_space, count)), out_sh...]
where the time goes in v6:
time: 55.1 us; the launch traced here: 54.7 us
  Pallas kernels  54.1 us (98%)
  between operations  0.64 us (1%)
    pallas_call x1, Pallas kernels, body(): pl.pallas_call(functools.partial(kernel, (n_seg, n_space, count)), out_sh...  53 us

profile of v6, /device:TPU:1, one launch (start us, length us, event | category | flops | bytes accessed | tf_op | source)
XLA Modules:
  0.0 54.7 jit_solution(7645579238447071772)
XLA Ops:
  0.6 53.0 %shard_map.67 = (f32[25,3,4,8,128]{4,3,2,1,0:T(8,128)S(1)}, f32[1,24]{1,0:T(1,128)S(1)}, f32[1,24]{1,0:T(1,128)S(1)}) custom-call(f32[1,25,3,4,8,128]{5,4,3,2,1,0:T(8,128)} %tang.1, f32[1,4,3,4,8,128]{5,4,3,2,1,0:T(8,128)} %flow.1, f32[1,4,8,128]{3,2,1,0:T(8,128)} %visc.1, f32[1,3,4,8,128]{4,3,2,1,0:T(8,128)} %src.1), custom_call_target="tpu_custom_call" | custom-call | tf_op jit(solution)/shard_map/pallas_call | solution.py:438
  53.6 1.1 %shard_map.68 = (f32[1,25,3,4,8,128]{5,4,3,2,1,0:T(8,128)}, f32[1,24]{1,0:T(1,128)}, f32[1,24]{1,0:T(1,128)}) custom-call(f32[25,3,4,8,128]{4,3,2,1,0:T(8,128)S(1)} %get-tuple-element.6.handed_in, f32[1,24]{1,0:T(1,128)S(1)} %get-tuple-element.7.growth_in, f32[1,24]{1,0:T(1,128)S(1)} %get-tuple-element.8.proj_in), custom_call_target="tpu_custom_call" | custom-call | tf_op jit(solution)/shard_map/pallas_call | solution.py:486

commit v7 on v6

--- a/solution.py
+++ b/solution.py
@@ -101,7 +101,7 @@
     ext, mid, flowx, viscx, srcx, coef, tmp_a, tmp_b, stepped, prev,
     accs, gram, spread, part_y, part_z, part_p, logs,
     local_sems, halo_send, halo_recv, side_send, side_recv,
-    shift_sems, y_send, y_recv, z_send, z_recv, p_send, p_recv,
+    shift_sems, y_sems, z_sems, p_sems,
     log_send, log_recv, rounds,
 ):
     n_seg, n_space, count = sizes
@@ -150,6 +150,12 @@
             device_id=device, device_id_type=MESH,
         )
 
+    def landed(size, sem):
+        remote(size, size, halo_send.at[0], sem, left).wait_recv()
+
+    def gone(size, sem):
+        remote(size, size, sem, halo_recv.at[0, 0], left).wait_send()
+
     def tag(k):
         return k.start if isinstance(k, pl.Slice) else k
 
@@ -158,15 +164,15 @@
             remote(ext.at[k, :, pl.ds(SLAB, HALO)], ext.at[k, :, pl.ds(0, HALO)],
                    halo_send.at[0], halo_recv.at[0, tag(k)], right),
             remote(ext.at[k, :, pl.ds(HALO, HALO)], ext.at[k, :, pl.ds(SLAB + HALO, HALO)],
-                   halo_send.at[1], halo_recv.at[1, tag(k)], left),
+                   halo_send.at[1], halo_recv.at[0, tag(k)], left),
         ]
 
     def second(k):
         return [
             remote(mid.at[k, :, pl.ds(SLAB, HALO)], mid.at[k, :, pl.ds(0, HALO)],
-                   halo_send.at[2], halo_recv.at[2, tag(k)], right),
+                   halo_send.at[2], halo_recv.at[1, tag(k)], right),
             remote(mid.at[k, :, pl.ds(HALO, HALO)], mid.at[k, :, pl.ds(SLAB + HALO, HALO)],
-                   halo_send.at[3], halo_recv.at[3, tag(k)], left),
+                   halo_send.at[3], halo_recv.at[1, tag(k)], left),
         ]
 
     sides = []
@@ -216,8 +222,7 @@
                 dst[c, lo - base : hi - base] = driven + DT * srcx[c, lo:hi]
 
     def start(k):
-        for copy in halo(k):
-            copy.wait_recv()
+        landed(ext.at[k, :, pl.ds(0, 2 * HALO)], halo_recv.at[0, k])
 
         @pl.when(k + AHEAD < total)
         def _():
@@ -230,8 +235,7 @@
             copy.start()
 
     def finish(k):
-        for copy in second(k):
-            copy.wait_recv()
+        landed(mid.at[k, :, pl.ds(0, 2 * HALO)], halo_recv.at[1, k])
         advance(k, 2, mid.at[k], tmp_b, 0)
         advance(k, 3, tmp_b, stepped.at[k], HALO)
         shift(k).start()
@@ -289,21 +293,20 @@
     part_y[y] = packed * (1.0 / cells)
 
     def exchange_y(d):
-        return remote(part_y.at[y], part_y.at[y], y_send.at[d], y_recv.at[y], along_y(d))
+        return remote(part_y.at[y], part_y.at[y], y_sems.at[0], y_sems.at[1], along_y(d))
 
     def exchange_z(d):
-        return remote(part_z.at[z], part_z.at[z], z_send.at[d], z_recv.at[z], along_z(d))
+        return remote(part_z.at[z], part_z.at[z], z_sems.at[0], z_sems.at[1], along_z(d))
 
     def exchange_p(d):
-        return remote(part_z.at[z], part_p.at[z], p_send.at[d], p_recv.at[z], along_z(d, 1))
+        return remote(part_z.at[z], part_p.at[z], p_sems.at[0], p_sems.at[1], along_z(d, 1))
 
     def arrived(slot, sems, position):
-        remote(slot.at[position], slot.at[position], y_send.at[0], sems.at[position], left).wait_recv()
+        remote(slot.at[position], slot.at[position], y_sems.at[0], sems.at[position], left).wait_recv()
 
     for d in range(1, ROW):
         exchange_y(d).start()
-    for d in range(1, ROW):
-        arrived(part_y, y_recv, lax.rem(y + d, ROW))
+    landed(part_y.at[pl.ds(0, ROW - 1)], y_sems.at[1])
     part_z[z] = part_y[0] + part_y[1] + part_y[2] + part_y[3]
     far_first = sorted(range(depth), key=lambda d: -min(d, depth - d))
     for d in far_first[:-1]:
@@ -317,10 +320,8 @@
     for copy in halo(every) + second(every):
         copy.wait_send()
     shift(every).wait()
-    for d in range(1, ROW):
-        exchange_y(d).wait_send()
-    for d in range(1, depth):
-        arrived(part_z, z_recv, lax.rem(z + d, depth))
+    gone(part_y.at[pl.ds(0, ROW - 1)], y_sems.at[0])
+    landed(part_z.at[pl.ds(0, depth - 1)], z_sems.at[1])
 
     def unpack(slots):
         sums = slots[0]
@@ -346,10 +347,8 @@
         def _():
             exchange_log(d).start()
 
-    for d in range(1, depth):
-        exchange_z(d).wait_send()
-    for d in range(depth):
-        arrived(part_p, p_recv, lax.rem(z + d, depth))
+    gone(part_z.at[pl.ds(0, depth - 1)], z_sems.at[0])
+    landed(part_p, p_sems.at[1])
     inner = jnp.where(rows == lanes, mine[:, count : count + 1] * scale, 0.0)
     proj[...] = jnp.sum(inner, axis=0, keepdims=True)[:, :count]
 
@@ -397,8 +396,7 @@
 
     growth[...] = sums[0:1, :count]
 
-    for d in range(depth):
-        exchange_p(d).wait_send()
+    gone(part_p, p_sems.at[0])
     for d in range(1, n_seg):
 
         @pl.when(seg + d < n_seg)
@@ -464,16 +462,13 @@
             pltpu.VMEM((n_seg, 8, 128), f32),
             dma((4,)),
             dma((4,)),
-            dma((4, total)),
+            dma((2, total)),
             dma((2, 6)),
             dma((2, 6)),
             dma((2,)),
-            dma((ROW,)),
-            dma((ROW,)),
-            dma((depth,)),
-            dma((depth,)),
-            dma((depth,)),
-            dma((depth,)),
+            dma((2,)),
+            dma((2,)),
+            dma((2,)),
             dma((n_seg,)),
             dma((n_seg,)),
             pltpu.SemaphoreType.REGULAR((4,)),

time: 55.1 us -> 54.3 us (0.985)
  Pallas kernels: 54.1 us -> 53.3 us
    pallas_call x1, Pallas kernels: 53 us -> 52.2 us  [body(): pl.pallas_call(functools.partial(kernel, (n_seg, n_space, count)), out_sh...]
where the time goes in v7:
time: 54.3 us; the launch traced here: 53.9 us
  Pallas kernels  53.3 us (98%)
  between operations  0.64 us (1%)
    pallas_call x1, Pallas kernels, body(): pl.pallas_call(functools.partial(kernel, (n_seg, n_space, count)), out_sh...  52.2 us
    pallas_call x1, Pallas kernels, body(): pl.pallas_call(deliver, out_shape=(jax.ShapeDtypeStruct(tangents.shape, f...  1.09 us

profile of v7, /device:TPU:1, one launch (start us, length us, event | category | flops | bytes accessed | tf_op | source)
XLA Modules:
  0.0 53.9 jit_solution(7781076848145570012)
XLA Ops:
  0.6 52.2 %shard_map.67 = (f32[25,3,4,8,128]{4,3,2,1,0:T(8,128)S(1)}, f32[1,24]{1,0:T(1,128)S(1)}, f32[1,24]{1,0:T(1,128)S(1)}) custom-call(f32[1,25,3,4,8,128]{5,4,3,2,1,0:T(8,128)} %tang.1, f32[1,4,3,4,8,128]{5,4,3,2,1,0:T(8,128)} %flow.1, f32[1,4,8,128]{3,2,1,0:T(8,128)} %visc.1, f32[1,3,4,8,128]{4,3,2,1,0:T(8,128)} %src.1), custom_call_target="tpu_custom_call" | custom-call | tf_op jit(solution)/shard_map/pallas_call | solution.py:436
  52.8 1.1 %shard_map.68 = (f32[1,25,3,4,8,128]{5,4,3,2,1,0:T(8,128)}, f32[1,24]{1,0:T(1,128)}, f32[1,24]{1,0:T(1,128)}) custom-call(f32[25,3,4,8,128]{4,3,2,1,0:T(8,128)S(1)} %get-tuple-element.6.handed_in, f32[1,24]{1,0:T(1,128)S(1)} %get-tuple-element.7.growth_in, f32[1,24]{1,0:T(1,128)S(1)} %get-tuple-element.8.proj_in), custom_call_target="tpu_custom_call" | custom-call | tf_op jit(solution)/shard_map/pallas_call | solution.py:481
